TPU v7x, 128 devices: a whole 4x4x4 slice. The times are simulated.
128 devices in a mesh: node: 16 (over x_hi, z, core), local: 8 (over y, x_lo).
Axes of the slice: x: 4 (x_hi: 2, x_lo: 2; x = x_hi * 2 + x_lo), y: 4, z: 4, core: 2. Of those that a mesh axis runs over, the one named last changes fastest.
Arguments:
- tokens: bfloat16 [16384, 8192], P(('node', 'local')), may hold values from -24 to 24
- upstream: bfloat16 [16384, 8192], P(('node', 'local')), may hold values from -1.5 to 1.5
- router_probs: float32 [16384, 64], P(('node', 'local')), may hold values from 0.01 to 0.3
- expert_ids: int32 [16384, 2], P(('node', 'local')), may hold values from 0 to 63, as said below
- slot_index: int32 [16384, 2], P(('node', 'local')), may hold values from -1 to 3, as said below
- w_in: bfloat16 [2, 8192, 16384], P(None, 'local', 'node'), may hold values from -0.0625 to 0.0625
- w_out: bfloat16 [2, 16384, 8192], P(None, 'node', 'local'), may hold values from -0.046875 to 0.046875
- router_weight: bfloat16 [8192, 64], replicated, may hold values from -0.125 to 0.125
Outputs:
- token_grads: bfloat16 [16384, 8192], P(('node', 'local'))
- w_in_grad: bfloat16 [2, 8192, 16384], P(None, 'local', 'node')
- w_out_grad: bfloat16 [2, 16384, 8192], P(None, 'node', 'local')
- router_grad: float32 [8192, 64], P(('node', 'local'))
Inputs may be any that keep to these rules, and one draw needn't show every extreme that they name: `expert_ids`: each token names two different experts. `slot_index`: an assignment to an expert under 2 has as slot its rank among its device's 128 tokens' assignments to that expert, in an order drawn at random, and -1 when that rank is 4 or more; every assignment to another expert has -1. In every draw some expert under 2 fills all 4 slots from every device.
All inputs are finite; a program needn't handle non-finite values.
Results may differ from a plain program's by a relative error of at most 0.017.
Values may be sent and summed in bfloat16 or wider, within the bound.
No kernel may reach another device: no remote copies, remote signals or barrier semaphores. Data moves between devices by JAX's collectives and lax.ppermute only.
A program may use at most 128 MiB of HBM per device.

v0:
```python
import math

import jax
import jax.numpy as jnp
from jax import lax
from jax.sharding import PartitionSpec as P

CAP = 4


root_two_pi = math.sqrt(2.0 / math.pi)
cubic_coef = 0.044715


def gelu_pair(pre):
    inner = root_two_pi * (pre + cubic_coef * pre * pre * pre)
    tangent = jnp.tanh(inner)
    value = 0.5 * pre * (1.0 + tangent)
    slope = 0.5 * (1.0 + tangent) + 0.5 * pre * (1.0 - tangent * tangent) * root_two_pi * (
        1.0 + 3.0 * cubic_coef * pre * pre
    )
    return (value, slope)


def contract(left, right, left_dim, right_dim):
    return lax.dot_general(
        left, right, (((left_dim,), (right_dim,)), ((), ())), preferred_element_type=jnp.float32
    )


def hidden_step(pre, upw, gate_wide):
    value, slope = gelu_pair(pre)
    act = value.astype(jnp.bfloat16)
    pre_grad = (gate_wide * upw * slope).astype(jnp.bfloat16)
    scores = jnp.sum(act.astype(jnp.float32) * upw, axis=2)
    return (act, pre_grad, scores)


def local(tokens, upstream, router_probs, expert_ids, slot_index, w_in, w_out, router_weight):
    token_count, model_width = tokens.shape
    flight = w_in.shape[0]
    feature_width = w_in.shape[1]
    capacity = CAP
    node_count = lax.axis_size("node")
    local_count = lax.axis_size("local")
    span = local_count * capacity
    is_kept = slot_index >= 0
    target = jnp.where(is_kept, expert_ids * capacity + slot_index, -1)
    slot_iota = jnp.arange(flight * capacity, dtype=jnp.int32)
    slot_hits = slot_iota[:, None, None] == target[None, :, :]
    placing = jnp.any(slot_hits, axis=2).astype(jnp.bfloat16)
    send_in = jnp.dot(placing, tokens, preferred_element_type=jnp.float32).astype(jnp.bfloat16)
    send_up = jnp.dot(placing, upstream, preferred_element_type=jnp.float32).astype(jnp.bfloat16)
    chosen = jnp.take_along_axis(router_probs, expert_ids, axis=1)
    send_gate = jnp.sum(
        jnp.where(slot_hits, chosen[None, :, :], jnp.zeros((), jnp.float32)), axis=(1, 2)
    ).astype(jnp.bfloat16)
    full_in, full_up, full_gate = (
        lax.all_gather(
            send_in.reshape(flight, 1, capacity, model_width), "node", axis=1, tiled=True
        ),
        lax.all_gather(
            send_up.reshape(flight, 1, capacity, model_width), "node", axis=1, tiled=True
        ),
        lax.all_gather(send_gate.reshape(flight, 1, capacity, 1), "node", axis=1, tiled=True),
    )
    in_block = full_in.reshape(flight, node_count, 1, capacity, local_count, feature_width)
    up_block = full_up.reshape(flight, node_count, 1, capacity, local_count, feature_width)
    gate_block = jnp.broadcast_to(
        full_gate.reshape(flight, node_count, 1, capacity, 1, 1),
        (flight, node_count, 1, capacity, local_count, 1),
    )
    got_in, got_up, got_gate = (
        lax.all_to_all(in_block, "local", split_axis=4, concat_axis=2, tiled=True),
        lax.all_to_all(up_block, "local", split_axis=4, concat_axis=2, tiled=True),
        lax.all_to_all(gate_block, "local", split_axis=4, concat_axis=2, tiled=True),
    )
    rows_in = got_in.reshape(flight, -1, feature_width)
    rows_up = got_up.reshape(flight, -1, feature_width)
    gate_wide = got_gate.reshape(flight, -1).astype(jnp.float32)[:, :, None]
    pre_part = jnp.einsum("erd,edf->erf", rows_in, w_in, preferred_element_type=jnp.float32)
    upw_part = jnp.einsum("erd,efd->erf", rows_up, w_out, preferred_element_type=jnp.float32)
    pre, upw = lax.psum((pre_part, upw_part), "local")
    act, pre_grad, score_part = hidden_step(pre, upw, gate_wide)
    out_grad = (gate_wide * rows_up.astype(jnp.float32)).astype(jnp.bfloat16)
    w_out_grad = jnp.einsum(
        "erf,erd->efd", act, out_grad, preferred_element_type=jnp.float32
    ).astype(jnp.bfloat16)
    w_in_grad = jnp.einsum(
        "erd,erf->edf", rows_in, pre_grad, preferred_element_type=jnp.float32
    ).astype(jnp.bfloat16)
    row_terms = jnp.einsum("erf,edf->erd", pre_grad, w_in, preferred_element_type=jnp.float32)
    back_terms, back_scores = (
        lax.psum_scatter(
            row_terms.reshape(flight, node_count, span, feature_width),
            "node",
            scatter_dimension=1,
            tiled=True,
        ),
        lax.psum_scatter(
            score_part.reshape(flight, node_count, span), "node", scatter_dimension=1, tiled=True
        ),
    )
    row_grads = back_terms.astype(jnp.bfloat16).reshape(
        flight, local_count, capacity, 1, feature_width
    )
    home_rows = lax.all_to_all(row_grads, "local", split_axis=1, concat_axis=3, tiled=True).reshape(
        flight * capacity, model_width
    )
    combined = contract(placing, home_rows, 0, 0)
    own_scores = lax.dynamic_slice_in_dim(
        back_scores.reshape(flight, local_count, capacity), lax.axis_index("local"), 1, 1
    ).reshape(-1)
    safe_slot = jnp.where(is_kept, target, 0)
    gate_grad = jnp.where(is_kept, own_scores[safe_slot], jnp.zeros((), jnp.float32))
    expert_count = router_probs.shape[1]
    expert_iota = jnp.arange(expert_count, dtype=jnp.int32)
    matches = expert_ids[:, :, None] == expert_iota[None, None, :]
    prob_grad = jnp.sum(
        jnp.where(matches, gate_grad[:, :, None], jnp.zeros((), jnp.float32)), axis=1
    )
    centred = prob_grad - jnp.sum(router_probs * prob_grad, axis=1, keepdims=True)
    logit_grad = (router_probs * centred).astype(jnp.bfloat16)
    router_grad = lax.psum_scatter(
        contract(tokens, logit_grad, 0, 0), ("node", "local"), scatter_dimension=0, tiled=True
    )
    router_part = contract(logit_grad, router_weight, 1, 1)
    token_grads = (combined + router_part).astype(jnp.bfloat16)
    return (token_grads, w_in_grad, w_out_grad, router_grad)


def solution(mesh):
    in_specs = (
        P(("node", "local"), None),
        P(("node", "local"), None),
        P(("node", "local"), None),
        P(("node", "local"), None),
        P(("node", "local"), None),
        P(None, "local", "node"),
        P(None, "node", "local"),
        P(),
    )
    out_specs = (
        P(("node", "local"), None),
        P(None, "local", "node"),
        P(None, "node", "local"),
        P(("node", "local"), None),
    )
    return jax.shard_map(local, mesh=mesh, in_specs=in_specs, out_specs=out_specs, check_vma=False)
```

profile of v0, /device:TPU:16, one launch (start us, length us, event | category | flops | bytes accessed | tf_op | source)
XLA Modules:
  0.0 1250.4 jit_solution(814197240158802227)
XLA Ops:
  7.2 0.8 add_select_fusion
  8.1 2.0 convolution_convert_fusion.1
  10.0 0.7 reshape.92
  10.9 0.4 convolution_convert_fusion
  11.2 0.7 reshape.95
  12.0 48.9 %all-gather.3.cloned.1.call-done = bf16[2,16,4,8192]{3,2,0,1:T(4,128)(2,1)} async-done(((bf16[2,1,4,8192]{3,2,0,1:T(4,128)(2,1)}), bf16[2,16,4,8192]{3,2,0,1:T(4,128)(2,1)}) %all-gather.3.cloned.1.call-update) | async-done | bytes 2097168 | tf_op jit(solution)/shard_map/all_gather | solution.py:62
  60.9 4.5 reshape.93
  65.3 4.5 copy.203
  69.9 4.8 all-to-all-start.1
  74.7 39.0 %all-gather.5.cloned.1.call-done = bf16[2,16,4,8192]{3,2,0,1:T(4,128)(2,1)} async-done(((bf16[2,1,4,8192]{3,2,0,1:T(4,128)(2,1)}), bf16[2,16,4,8192]{3,2,0,1:T(4,128)(2,1)}) %all-gather.5.cloned.1.call-update) | async-done | bytes 2097168 | tf_op jit(solution)/shard_map/all_gather | solution.py:59
  113.7 4.5 reshape.96
  118.1 4.5 copy.205
  122.7 5.5 all-to-all-start.2
  128.1 4.0 copy.204
  132.2 4.0 reshape.94
  136.1 16.8 %all-to-all-done.2 = bf16[2,16,1,4,8,1024]{5,3,1,0,2,4:T(4,128)(2,1)} async-done(((bf16[2,16,1,4,8,1024]{5,3,1,0,2,4:T(4,128)(2,1)}), bf16[2,16,1,4,8,1024]{5,3,1,0,2,4:T(4,128)(2,1)}, u32[]{:S(2)}, u32[]{:S(2)}) %all-to-all-start.2) | async-done | bytes 2097184 | tf_op jit(solution)/shard_map/all_to_all | solution.py:74
  152.9 4.0 copy.206
  157.0 4.0 reshape.97
  161.0 7.4 fusion.12
  168.3 4.4 fusion.13
  172.7 0.2 reduce-scatter.5.cloned.1.call-start
  173.0 0.4 copy-done.5
  173.5 0.1 reshape.121
  173.7 2.0 gather_fusion
  176.1 23.1 %all_gather.9 = bf16[2,16,4,1]{2,0,3,1:T(2,128)(2,1)S(1)} all-gather(bf16[2,1,4,1]{2,0,3,1:T(2,128)(2,1)S(1)} %convert_element_type.67), channel_id=1, replica_groups=mesh['node'=16,'local'=8] {'node'}, dimensions={1}, use_global_device_ids=true | all-gather | bytes 272 | tf_op jit(solution)/shard_map/all_gather | solution.py:65
  199.3 9.4 all_to_all.54
  208.6 0.2 copy.202
  209.0 304.9 %all-reduce.4.cloned.1.call-done = (f32[2,512,1024]{2,1,0:T(8,128)}, f32[2,512,1024]{2,1,0:T(8,128)}) async-done(((f32[2,512,1024]{2,1,0:T(8,128)}, f32[2,512,1024]{2,1,0:T(8,128)}), (f32[2,512,1024]{2,1,0:T(8,128)}, f32[2,512,1024]{2,1,0:T(8,128)})) %all-reduce.4.cloned.1.call-update) | async-done | bytes 8388624 | tf_op jit(solution)/shard_map/psum | solution.py:83
  513.8 5.9 multiply_reduce_fusion
  519.8 2.4 fusion.14
  522.1 2.5 copy.207
  524.8 0.6 copy-done.9
  525.3 0.6 dynamic-slice
  526.0 69.5 %all-reduce = f32[2,16,32]{2,0,1:T(2,128)S(1)} all-reduce(f32[2,16,32]{2,0,1:T(2,128)S(1)} %copy.211), channel_id=3, replica_groups=mesh['node'=16,'local'=8] {'node'}, use_global_device_ids=true, to_apply=%region_6.7.clone | all-reduce | flops 1024 | bytes 8192
  595.5 0.6 constant_dynamic-slice_fusion
  596.4 0.7 fusion.11
  597.1 5.0 fusion.10
  602.1 1.7 convolution_bitcast_fusion
  603.9 3.8 copy.217
  607.7 7.8 convolution_convert_fusion.2
  615.5 1.0 convert_element_type.75
  616.5 0.8 copy.208
  617.3 5.2 all-to-all-start.3
  622.5 6.6 convolution_convert_fusion.3
  629.3 0.7 fusion.15
  630.1 0.3 copy-done.4
  630.4 2.1 fusion
  632.5 611.4 %reduce-scatter.7.cloned.1.call-done = f32[64,64]{1,0:T(8,128)} async-done(((f32[8192,64]{1,0:T(8,128)}), f32[64,64]{1,0:T(8,128)}) %reduce-scatter.7.cloned.1.call-update) | async-done | bytes 16400
  (51 shorter events, 1.5 us)
Async XLA Ops:
  7.2 3.7 copy-start
  7.2 53.7 %all-gather.3.cloned.1.call-start = ((), (), s32[]{:S(2)}) async-start(), calls=%async_computation.6 | async-start | bytes 2228224 | tf_op jit(solution)/shard_map/all_gather | solution.py:62
  10.8 102.9 %all-gather.5.cloned.1.call-start = ((), (), s32[]{:S(2)}) async-start(), calls=%async_computation.7 | async-start | bytes 2228224 | tf_op jit(solution)/shard_map/all_gather | solution.py:59
  69.9 52.8 %all-to-all-start.1 = ((bf16[2,16,1,4,8,1024]{5,3,1,0,2,4:T(4,128)(2,1)}), bf16[2,16,1,4,8,1024]{5,3,1,0,2,4:T(4,128)(2,1)}, u32[]{:S(2)}, u32[]{:S(2)}) async-start(bf16[2,16,1,4,8,1024]{5,3,1,0,2,4:T(4,128)(2,1)} %copy.203), calls=%async_computation.1 | async-start | bytes 4194304 | tf_op jit(solution)/shard_map/all_to_all | solution.py:75
  122.7 30.3 %all-to-all-start.2 = ((bf16[2,16,1,4,8,1024]{5,3,1,0,2,4:T(4,128)(2,1)}), bf16[2,16,1,4,8,1024]{5,3,1,0,2,4:T(4,128)(2,1)}, u32[]{:S(2)}, u32[]{:S(2)}) async-start(bf16[2,16,1,4,8,1024]{5,3,1,0,2,4:T(4,128)(2,1)} %copy.205), calls=%async_computation.2 | async-start | bytes 4194304 | tf_op jit(solution)/shard_map/all_to_all | solution.py:74
  128.1 385.7 %all-reduce.4.cloned.1.call-start = ((), (), s32[]{:S(2)}) async-start(), calls=%async_computation.10 | async-start | bytes 16777216 | tf_op jit(solution)/shard_map/psum | solution.py:83
  161.0 7.4 copy-start.2
  161.0 7.4 copy-start.7
  172.7 0.7 copy-start.5
  172.7 0.9 copy-start.1
  172.7 442.8 %reduce-scatter.5.cloned.1.call-start = ((), (), s32[]{:S(2)}) async-start(), calls=%async_computation.8 | async-start | bytes 4456448 | tf_op jit(solution)/shard_map/reduce_scatter | solution.py:94
  513.8 5.9 copy-start.8
  519.7 2.4 copy-start.3
  524.7 0.7 copy-start.9
  524.7 72.4 %copy-start.6 = (s32[128,2]{0,1:T(2,128)S(1)}, s32[128,2]{0,1:T(2,128)}, u32[]{:S(2)}) copy-start(s32[128,2]{0,1:T(2,128)} %param.12) | copy-start | bytes 3076
  524.7 719.2 %reduce-scatter.7.cloned.1.call-start = ((), (), s32[]{:S(2)}) async-start(), calls=%async_computation.9 | async-start | bytes 4227072
  617.3 11.9 all-to-all-start.3
  629.2 1.2 copy-start.4
Sparse Core Ops, SparseCore 0:
  11.1 49.7 all-gather.2
  63.9 49.6 all-gather.4
  172.9 340.8 all-reduce.3
  524.8 81.6 reduce-scatter.4
  609.4 634.4 reduce-scatter.6
where the time goes:
time: 1260 us; the launch traced here: 1250 us
  waiting for transfers between devices  1020 us (81%)
  blocking collectives  102 us (8%)
  local copies, waits for them, and re-layouts  49.2 us (4%)
  matrix products  35.5 us (3%)
  starting transfers between devices  15.9 us (1%)
  between operations  13.9 us (1%)
  other arithmetic  12.9 us (1%)
    unnamed x6, waiting for transfers between devices  611 us
    psum x1, waiting for transfers between devices, local(): pre, upw = lax.psum((pre_part, upw_part), 'local')  305 us
    unnamed x1, blocking collectives  69.5 us
    all_gather x1, waiting for transfers between devices, local(): lax.all_gather(send_up.reshape(flight, 1, capacity, model_width), 'node',...  48.9 us
    all_gather x1, waiting for transfers between devices, local(): lax.all_gather(send_in.reshape(flight, 1, capacity, model_width), 'node',...  39 us
  transfers between devices with their start and end apart: 8, of which 5 were waited for; matrix products, arithmetic and copies ran while one was open for 5% of the time, Pallas kernels for 0%

commit v1 on v0

v1 whole, which is shorter than its diff:
```python
import math

import jax
import jax.numpy as jnp
from jax import lax
from jax.experimental import pallas as pl
from jax.experimental.pallas import tpu as pltpu
from jax.sharding import PartitionSpec as P

CAP = 4


root_two_pi = math.sqrt(2.0 / math.pi)
cubic_coef = 0.044715
bf16 = jnp.bfloat16
f32 = jnp.float32


def gelu_pair(pre):
    inner = root_two_pi * (pre + cubic_coef * pre * pre * pre)
    tangent = jnp.tanh(inner)
    value = 0.5 * pre * (1.0 + tangent)
    slope = 0.5 * (1.0 + tangent) + 0.5 * pre * (1.0 - tangent * tangent) * root_two_pi * (
        1.0 + 3.0 * cubic_coef * pre * pre
    )
    return (value, slope)


def contract(left, right, left_dim, right_dim):
    return lax.dot_general(
        left, right, (((left_dim,), (right_dim,)), ((), ())), preferred_element_type=f32
    )


same_core = [[place * 2 + core for place in range(8)] for core in range(2)]


def send_core(value):
    return lax.ppermute(value, "node", [(i, i ^ 1) for i in range(16)])


def send_x_hi(value):
    return lax.ppermute(value, "node", [(i, i ^ 8) for i in range(16)])


def send_x(value):
    return lax.ppermute(value, "local", [(i, i ^ 1) for i in range(8)])


def trade_places(blocks):
    return lax.all_to_all(blocks, "node", 0, 0, tiled=True, axis_index_groups=same_core)


def send_z(value, step):
    pairs = [(i, (i // 8 * 4 + (i // 2 + step) % 4) * 2 + i % 2) for i in range(16)]
    return lax.ppermute(value, "node", pairs)


def send_y(value, step):
    return lax.ppermute(value, "local", [(i, (i // 2 + step) % 4 * 2 + i % 2) for i in range(8)])


def ring(value, send):
    return [value] + [send(value, 4 - step) for step in range(1, 4)]


def turn(start):
    places = jnp.arange(4)
    return (places[:, None] + start) % 4 == places[None, :]


def turned(value, hit, axis):
    value = jnp.moveaxis(value, axis, 0)
    hit = hit.reshape((4, 4) + (1,) * (value.ndim - 1))
    return jnp.moveaxis(jnp.sum(jnp.where(hit, value[None], jnp.zeros((), f32)), axis=1), 0, axis)


def trade_all(value):
    return lax.all_to_all(value, ("node", "local"), 0, 0, tiled=True)


def spread(value, count):
    return jnp.broadcast_to(value[None], (count,) + value.shape)


def after(value, *others):
    return lax.optimization_barrier((value,) + others)[0]


def together(*values):
    return lax.optimization_barrier(values)


def up(value):
    return value.astype(f32)


def pick(value, index, axis):
    return lax.dynamic_index_in_dim(value, index, axis, keepdims=False)


def join_x(mine, other, x, axis):
    return jnp.stack([jnp.where(x == 0, mine, other), jnp.where(x == 0, other, mine)], axis=axis)


def matmul(left, right, left_dim=1, right_dim=0):
    return contract(left, right, left_dim, right_dim)


tile = 256
room = 58 * 1024 * 1024


def call(kernel, grid, in_specs, out_specs, out_shape, flops, scratch=(), aliases=None):
    return pl.pallas_call(
        kernel,
        grid=grid,
        in_specs=in_specs,
        out_specs=out_specs,
        out_shape=out_shape,
        scratch_shapes=list(scratch),
        input_output_aliases=aliases or {},
        compiler_params=pltpu.CompilerParams(vmem_limit_bytes=room),
        cost_estimate=pl.CostEstimate(flops=flops, bytes_accessed=flops // 256, transcendentals=0),
    )


def row_specs():
    return [pl.BlockSpec((8, 32, 1024), lambda j, k=k: (0, k, 0)) for k in (0, 1, 0, 1)]


scalar_spec = pl.BlockSpec(memory_space=pltpu.SMEM)


step_width = 256


def weight_specs(e):
    return [
        pl.BlockSpec((1, 1024, step_width), lambda j: (e, 0, j)),
        pl.BlockSpec((1, step_width, 1024), lambda j: (e, j, 0)),
    ]


def projections(refs, rows):
    into, out_of = refs[4:]

    @pl.when(pl.program_id(0) == 0)
    def _():
        for part in range(4):
            half = part // 2 * 256
            rows[part % 2, half : half + 256, :] = refs[part][...].reshape(256, 1024)

    return matmul(rows[0], into[0]), matmul(rows[1], out_of[0], 1, 1)


def project_whole(near, far, w_in, w_out, e, spots):
    def kernel(at, *refs):
        outs, rows, parts = refs[6:10], refs[10], refs[11]
        for which, part in enumerate(projections(refs[:6], rows)):
            parts[:, which] = part.astype(bf16).reshape(4, 128, step_width)
        for step in range(4):
            outs[step][...] = parts[lax.rem(at[0] + step, 4)]

    return call(
        kernel,
        (1024 // step_width,),
        [scalar_spec] + row_specs() + weight_specs(e),
        [pl.BlockSpec((2, 128, step_width), lambda j: (0, 0, j))] * 4,
        [jax.ShapeDtypeStruct((2, 128, 1024), bf16)] * 4,
        2 * 2 * 512 * 1024 * 1024,
        [pltpu.VMEM((2, 512, 1024), bf16), pltpu.VMEM((4, 2, 128, step_width), bf16)],
    )(spots, near, near, far, far, w_in, w_out)


def project_split(near, far, w_in, w_out, e, spots):
    def kernel(at, *refs):
        kept, sent, rows = refs[6:]
        first = at[1] == 0
        for which, part in enumerate(projections(refs[:6], rows)):
            part = part.astype(bf16).reshape(4, 2, 64, step_width)
            low, high = part[:, 0], part[:, 1]
            mine, other = jnp.where(first, low, high), jnp.where(first, high, low)
            for y in range(4):
                place = lax.rem(y + 4 - at[0], 4)
                kept[place, which] = mine[y]
                sent[place, which] = other[y]

    return call(
        kernel,
        (1024 // step_width,),
        [scalar_spec] + row_specs() + weight_specs(e),
        [pl.BlockSpec((4, 2, 64, step_width), lambda j: (0, 0, 0, j))] * 2,
        [jax.ShapeDtypeStruct((4, 2, 64, 1024), bf16)] * 2,
        2 * 2 * 512 * 1024 * 1024,
        [pltpu.VMEM((2, 512, 1024), bf16)],
    )(spots, near, near, far, far, w_in, w_out)


def wide_specs(pieces, which):
    if len(pieces) == 4:
        return [pl.BlockSpec((1, 128, 1024), lambda j: (which, 0, 0))] * 4
    return [pl.BlockSpec((4, 1, 64, 1024), lambda j: (0, which, 0, 0))] * 2


def lay_rows(pieces, at, rows):
    for step in range(4):
        base = lax.rem(at[0] + step, 4) * 128
        if len(pieces) == 4:
            rows[pl.ds(pl.multiple_of(base, 128), 128), :] = pieces[step][0]
        else:
            for x, piece in ((at[1], pieces[0]), (1 - at[1], pieces[1])):
                rows[pl.ds(pl.multiple_of(base + x * 64, 64), 64), :] = piece[step, 0]


def row_terms_of(pieces, w_in, e, spots):
    count = len(pieces)
    wide = 512

    def kernel(at, *refs):
        grads, into, kept, sent, rows = refs[:count], *refs[count:]

        @pl.when(pl.program_id(0) == 0)
        def _():
            lay_rows(grads, at, rows)

        terms = matmul(rows[...], into[0], 1, 1)
        for step in range(4):
            z = lax.rem(at[2] + step, 4)
            for x_hi in range(2):
                block = (step * 2 + x_hi if e == 0 else x_hi * 4 + step) * 32
                kept[x_hi, z] = terms[block : block + 32]
                sent[x_hi, z] = terms[256 + block : 288 + block].astype(bf16)

    shape = (2, 4, 32, 1024)
    return call(
        kernel,
        (1024 // wide,),
        [scalar_spec]
        + wide_specs(pieces, 1)
        + [pl.BlockSpec((1, wide, 1024), lambda j: (e, j, 0))],
        [pl.BlockSpec((2, 4, 32, wide), lambda j: (0, 0, 0, j))] * 2,
        [jax.ShapeDtypeStruct(shape, f32), jax.ShapeDtypeStruct(shape, bf16)],
        2 * 512 * 1024 * 1024,
        [pltpu.VMEM((512, 1024), bf16)],
    )(spots, *pieces, w_in)


def weight_grads(near, far, gates, pieces, e, spots, earlier=()):
    count = len(pieces)

    def kernel(at, in0, up0, in1, up1, gate, *refs):
        acts, grads, refs = refs[:count], refs[count : 2 * count], refs[2 * count + len(earlier) :]
        into, out_of, act_rows, grad_rows, out_rows = refs
        j = pl.program_id(0)

        @pl.when(j == 0)
        def _():
            lay_rows(acts, at, act_rows)
            lay_rows(grads, at, grad_rows)
            for half, ups in enumerate((up0, up1)):
                part = slice(256 * half, 256 * half + 256)
                out_rows[part, :] = (
                    up(ups[...].reshape(256, 1024)) * gate[part, :]
                ).astype(bf16)

        columns = pl.ds(pl.multiple_of(j * tile, tile), tile)
        into[0] = (
            matmul(in0[:, :, columns].reshape(256, tile), grad_rows[:256, :], 0, 0)
            + matmul(in1[:, :, columns].reshape(256, tile), grad_rows[256:, :], 0, 0)
        ).astype(bf16)
        out_of[0] = matmul(act_rows[:, columns], out_rows[...], 0, 0).astype(bf16)

    return call(
        kernel,
        (1024 // tile,),
        [scalar_spec]
        + row_specs()
        + [pl.BlockSpec((512, 1), lambda j: (0, 0))]
        + wide_specs(pieces, 0)
        + wide_specs(pieces, 1)
        + [pl.BlockSpec(memory_space=pl.ANY)] * len(earlier),
        [pl.BlockSpec((1, tile, 1024), lambda j: (e, j, 0))] * 2,
        [jax.ShapeDtypeStruct((2, 1024, 1024), bf16)] * 2,
        2 * 2 * 512 * 1024 * 1024,
        [pltpu.VMEM((512, 1024), bf16)] * 3,
        {6 + 2 * count + i: i for i in range(len(earlier))},
    )(spots, near, near, far, far, gates, *pieces, *pieces, *earlier)


def local(tokens, upstream, router_probs, expert_ids, slot_index, w_in, w_out, router_weight):
    token_count, model_width = tokens.shape
    flight = w_in.shape[0]
    feature_width = w_in.shape[1]
    capacity = CAP
    expert_count = router_probs.shape[1]
    node = lax.axis_index("node")
    spot = lax.axis_index("local")
    x_hi, z, core, y, x = node // 8, node // 2 % 4, node % 2, spot // 2, spot % 2
    spots = jnp.stack([y, x, z]).astype(jnp.int32)
    span = 8 * capacity

    is_kept = slot_index >= 0
    target = jnp.where(is_kept, expert_ids * capacity + slot_index, -1)
    slot_iota = jnp.arange(flight * capacity, dtype=jnp.int32)
    slot_hits = slot_iota[:, None, None] == target[None, :, :]
    placing = jnp.any(slot_hits, axis=2).astype(bf16)
    send_in = jnp.dot(placing, tokens, preferred_element_type=f32).astype(bf16)
    send_up = jnp.dot(placing, upstream, preferred_element_type=f32).astype(bf16)
    slot_probs = jnp.dot(placing, router_probs.astype(bf16), preferred_element_type=f32)
    same = contract(placing, placing, 1, 1)
    twins = same[:, 4:]
    counted = 1 - jnp.where(slot_iota < 4, 0, jnp.sum(same[:, :4], axis=1))[:, None]
    facts = jnp.pad(
        jnp.concatenate([slot_probs, twins, counted], axis=1).astype(bf16), ((0, 8), (0, 59))
    )
    blocks = jnp.stack([send_in, send_up]).reshape(16, 8, feature_width).transpose(1, 0, 2)
    got = lax.all_to_all(
        jnp.concatenate([blocks, spread(facts, 8)], axis=2), "local", 0, 0, tiled=True
    )
    facts = (
        got[:, :8, feature_width:].reshape(8, flight, capacity, 128)
        .transpose(1, 0, 2, 3)
        .reshape(8, 8, 128)
        .transpose(1, 0, 2)
        .reshape(8, feature_width)
    )
    got = (
        got[:, :, :feature_width]
        .reshape(8, 2, flight, capacity, feature_width)
        .transpose(2, 1, 0, 3, 4)
        .reshape(4 * span, feature_width)
    )
    packets = [got[: 2 * span], jnp.concatenate([got[2 * span :], facts])]

    pair0 = join_x(packets[0], send_x_hi(packets[0]), x_hi, 0)
    ring1 = jnp.stack(ring(packets[1], send_z))
    pair0, ring1 = together(pair0, ring1)
    near1 = join_x(ring1, send_x_hi(ring1), x_hi, 0).reshape(8, -1, feature_width)
    near0 = jnp.stack(ring(pair0, send_z)).reshape(8, -1, feature_width)
    near0, near1, turns = together(near0, near1, turn(z))
    near, far = [near0, near1], [send_core(near0), send_core(near1)]
    facts = (
        jnp.stack([near1[:, 2 * span :], far[1][:, 2 * span :]])
        .reshape(16, 8, 8, 128)
        .transpose(0, 2, 1, 3)
        .reshape(16, flight, span, 128)
    )
    facts = [
        facts[:, 0].reshape(2, 2, 4, span, 128).transpose(0, 2, 1, 3, 4).reshape(-1, 128),
        facts[:, 1].reshape(-1, 128),
    ]
    gates = [up(facts[e][:, e : e + 1]) for e in range(flight)]

    kept1, sent1 = project_split(near[1], far[1], w_in, w_out, 1, spots)
    other1 = send_x(sent1)
    parts0 = project_whole(after(near[0], sent1), far[0], w_in, w_out, 0, spots)
    got0 = [send_y(parts0[step], step) for step in range(1, 4)]
    other1, got0 = together(other1, got0)
    half0 = (up(parts0[0]) + sum(up(part) for part in got0)).reshape(2, 2, 64, -1)
    half1 = [up(kept1[step]) + up(other1[step]) for step in range(4)]
    sent0, sent1 = together(
        pick(half0, 1 - x, 1).astype(bf16), [half1[step].astype(bf16) for step in range(1, 4)]
    )
    other0, got1 = together(
        send_x(sent0), [send_y(part, step + 1) for step, part in enumerate(sent1)]
    )
    sum0 = pick(half0, x, 1) + up(other0)
    sum1 = half1[0] + sum(up(part) for part in got1)
    scores, blocks = [], []
    for e, (pre, upw) in enumerate((sum0, sum1)):
        gate = lax.dynamic_slice_in_dim(gates[e], spot * 64, 64, 0)
        value, slope = gelu_pair(pre)
        act = value.astype(bf16)
        pre_grad = (gate * upw * slope).astype(bf16)
        scores.append(jnp.sum(up(act) * upw, axis=1))
        blocks.append(jnp.stack([act, pre_grad]))

    score = jnp.broadcast_to(jnp.stack(scores).reshape(1, 1, -1), (128, 1, 128))
    sent0, sent1, score = together(*blocks, score)
    other0, ring1, score = together(
        send_x(sent0), ring(sent1, send_y), score
    )
    pair0, ring1, score = together(
        join_x(sent0, other0, x, 1).reshape(2, 128, -1), jnp.stack(ring1), score
    )
    *wide, score = together(
        ring(pair0, send_y), [ring1, send_x(ring1)], trade_all(score)
    )
    score = jnp.sum(score.reshape(2, 4, 2, 8, flight, 2, span), axis=0)
    score = jnp.stack(
        [
            score[:, :, :, 0].reshape(4, 2, 2, 4, 2, span),
            score[:, :, :, 1].reshape(4, 2, 2, 2, 4, span).transpose(0, 1, 2, 4, 3, 5),
        ]
    )
    places = jnp.arange(4)
    hit = (places[:, None, None] + places[None, :, None]) % 4 == places[None, None, :]
    score = jnp.sum(
        jnp.where(
            hit.reshape(1, 4, 1, 1, 4, 4, 1, 1), score[:, :, :, :, :, None], jnp.zeros((), f32)
        ),
        axis=(1, 4),
    )
    score = jnp.stack(
        [score[:, 0, 0] + score[:, 1, 1], score[:, 0, 1] + score[:, 1, 0]], axis=1
    ).transpose(0, 1, 3, 2, 4)

    back = []
    for e in range(flight):
        kept, sent = row_terms_of(wide[e], w_in, e, spots)
        back.append(kept + up(send_core(sent)))
    sent = jnp.stack(back, axis=2).astype(bf16).reshape(8, flight, span, feature_width)
    row_grads = jnp.sum(up(trade_places(sent)), axis=0).astype(bf16)
    grads = ()
    for e in range(flight):
        grads = weight_grads(
            near[e], far[e], after(gates[e], sent), wide[e], e, spots, grads
        )
    w_in_grad, w_out_grad = grads

    home = lax.all_to_all(
        after(row_grads, w_in_grad).reshape(flight, 8, capacity, feature_width)
        .transpose(1, 0, 2, 3)
        .reshape(8, flight * capacity, feature_width),
        "local",
        0,
        0,
        tiled=True,
    )
    home = home.transpose(1, 0, 2).reshape(flight * capacity, model_width)

    own_scores = pick(pick(pick(score, core, 1), x_hi, 1), z, 1)
    own_scores = pick(own_scores.reshape(flight, 8, capacity), spot, 1).reshape(-1)
    score = turned(join_x(score[:, 0], score[:, 1], core, 1), turns, 3)
    swapped = score.transpose(0, 1, 3, 2, 4)
    score = [swapped[0], score[1]]

    router_terms = jnp.zeros((), f32)
    for e in range(flight):
        fact = up(facts[e])
        probs = fact[:, :expert_count]
        mine = jnp.arange(expert_count) == e
        grad = jnp.where(mine, score[e].reshape(-1, 1), jnp.zeros((), f32))
        if e == 0:
            twin = fact[:, expert_count : expert_count + capacity]
            twin = twin * jnp.repeat(swapped[1].reshape(-1, capacity), capacity, axis=0)
            twin = jnp.sum(twin, axis=1, keepdims=True)
            grad = jnp.where(jnp.arange(expert_count) == 1, twin, grad)
        else:
            grad = grad * fact[:, expert_count + capacity : expert_count + capacity + 1]
        centred = grad - jnp.sum(probs * grad, axis=1, keepdims=True)
        logits = (probs * centred).astype(bf16)
        columns = jnp.stack([near[e], far[e]])[:, :, :span]
        columns = lax.dynamic_slice_in_dim(columns, node * 64, 64, 3).reshape(-1, 64)
        router_terms = router_terms + contract(columns, logits, 0, 0)
    router_grad = lax.ppermute(
        router_terms, ("node", "local"), [(i, i % 8 * 16 + i // 8) for i in range(128)]
    )

    gate_grad = jnp.sum(
        jnp.where(slot_hits, own_scores[:, None, None], jnp.zeros((), f32)), axis=0
    )
    expert_iota = jnp.arange(expert_count, dtype=jnp.int32)
    matches = expert_ids[:, :, None] == expert_iota[None, None, :]
    prob_grad = jnp.sum(
        jnp.where(matches, gate_grad[:, :, None], jnp.zeros((), f32)), axis=1
    )
    centred = prob_grad - jnp.sum(router_probs * prob_grad, axis=1, keepdims=True)
    logit_grad = (router_probs * centred).astype(bf16)

    combined = contract(placing, home, 0, 0)
    router_part = contract(logit_grad, router_weight, 1, 1)
    token_grads = (combined + router_part).astype(bf16)
    return (token_grads, w_in_grad, w_out_grad, router_grad)


def solution(mesh):
    in_specs = (
        P(("node", "local"), None),
        P(("node", "local"), None),
        P(("node", "local"), None),
        P(("node", "local"), None),
        P(("node", "local"), None),
        P(None, "local", "node"),
        P(None, "node", "local"),
        P(),
    )
    out_specs = (
        P(("node", "local"), None),
        P(None, "local", "node"),
        P(None, "node", "local"),
        P(("node", "local"), None),
    )
    return jax.shard_map(local, mesh=mesh, in_specs=in_specs, out_specs=out_specs, check_vma=False)
```

time: 1260 us -> 219 us (0.17)
  waiting for transfers between devices: 1020 us -> 80.1 us
  blocking collectives: 102 us -> 11 us
  starting transfers between devices: 15.9 us -> 61.6 us
  local copies, waits for them, and re-layouts: 49.2 us -> 11.6 us
  Pallas kernels: 0 us -> 34.7 us
  matrix products: 35.5 us -> 5.41 us
    unnamed x6 -> x0, waiting for transfers between devices: 611 us -> none
    psum x1 -> x0, waiting for transfers between devices: 305 us -> none  [local(): pre, upw = lax.psum((pre_part, upw_part), 'local')]
    all_gather x2 -> x0, waiting for transfers between devices: 87.9 us -> none  [the longest x1 48.9 us: local(): lax.all_gather(send_up.reshape(flight, 1, capacity, model_width), 'node',...]
    unnamed x1 -> x0, blocking collectives: 69.5 us -> none
    ppermute x0 -> x29, waiting for transfers between devices: none -> 65.1 us  [the longest x12 39.4 us: send_y(): lax.ppermute(value, 'local', [(i, (i // 2 + step) % 4 * 2 + i % 2) for i...]
    ppermute x0 -> x29, starting transfers between devices: none -> 43.2 us  [the longest x12 20.6 us: send_y(): lax.ppermute(value, 'local', [(i, (i // 2 + step) % 4 * 2 + i % 2) for i...]
    pallas_call x0 -> x6, Pallas kernels: none -> 34.7 us  [the longest x2 13.3 us: weight_grads(): call(kernel, (1024 // tile,), [scalar_spec] + row_specs() + [pl.BlockSpec...]
    dot_general x7 -> x3, matrix products: 30.9 us -> 1.64 us  [the longest x1 0.88 us: local(): jnp.dot(placing, router_probs.astype(bf16), preferred_element_type=f32)]
  transfers between devices with their start and end apart: 8 -> 32, of which waited for: 5 -> 20; matrix products, arithmetic and copies ran while one was open for 5% -> 3% of each run, Pallas kernels for 0% -> 14%
where the time goes in v1:
time: 219 us; the launch traced here: 218 us
  waiting for transfers between devices  80.1 us (37%)
  starting transfers between devices  61.6 us (28%)
  Pallas kernels  34.7 us (16%)
  other arithmetic  12.6 us (6%)
  local copies, waits for them, and re-layouts  11.6 us (5%)
  blocking collectives  11 us (5%)
  matrix products  5.41 us (2%)
    ppermute x12, waiting for transfers between devices, send_y(): lax.ppermute(value, 'local', [(i, (i // 2 + step) % 4 * 2 + i % 2) for i...  39.4 us
    ppermute x12, starting transfers between devices, send_y(): lax.ppermute(value, 'local', [(i, (i // 2 + step) % 4 * 2 + i % 2) for i...  20.6 us
    ppermute x6, waiting for transfers between devices, send_z(): return lax.ppermute(value, 'node', pairs)  14.2 us
    all_to_all x1, waiting for transfers between devices, trade_all(): return lax.all_to_all(value, ('node', 'local'), 0, 0, tiled=True)  13.4 us
    pallas_call x2, Pallas kernels, weight_grads(): call(kernel, (1024 // tile,), [scalar_spec] + row_specs() + [pl.BlockSpec...  13.3 us
    all_to_all x1, blocking collectives, local(): lax.all_to_all(jnp.concatenate([blocks, spread(facts, 8)], axis=2), 'loca...  11 us
    ppermute x6, starting transfers between devices, send_z(): return lax.ppermute(value, 'node', pairs)  10.3 us
    all_to_all x1, starting transfers between devices, trade_all(): return lax.all_to_all(value, ('node', 'local'), 0, 0, tiled=True)  7.95 us
  transfers between devices with their start and end apart: 32, of which 20 were waited for; matrix products, arithmetic and copies ran while one was open for 3% of the time, Pallas kernels for 14%

profile of v1, /device:TPU:16, one launch (start us, length us, event | category | flops | bytes accessed | tf_op | source)
XLA Modules:
  0.0 218.5 jit_solution(9589201736563338531)
XLA Ops:
  3.1 1.2 copy-done.8
  5.2 11.0 %all_to_all.20 = bf16[8,16,1152]{2,1,0:T(8,128)(2,1)S(1)} all-to-all(bf16[8,16,1152]{2,1,0:T(8,128)(2,1)S(1)} %pad_maximum_fusion.6), channel_id=1, replica_groups=mesh['node'=16,'local'=8] {'local'}, dimensions={0} | all-to-all | bytes 589824 | tf_op jit(solution)/shard_map/all_to_all | solution.py:318
  16.5 2.8 %collective-permute-start = (bf16[64,1024]{1,0:T(8,128)(2,1)S(1)}, bf16[64,1024]{1,0:T(8,128)(2,1)S(1)}, u32[]{:S(2)}, u32[]{:S(2)}) collective-permute-start(bf16[64,1024]{1,0:T(8,128)(2,1)S(1)} %slice.122), channel_id=1, source_target_pairs={{0,64},{8,72},{16,80},{24,88},{32,96},{40,104},{48,112},{56,120},{... | collective-permute-start | bytes 393224 | tf_op jit(solution)/shard_map/ppermute | solution.py:43
  19.5 4.0 %collective-permute-start.2 = (bf16[72,1024]{1,0:T(8,128)(2,1)S(1)}, bf16[72,1024]{1,0:T(8,128)(2,1)S(1)}, u32[]{:S(2)}, u32[]{:S(2)}) collective-permute-start(bf16[72,1024]{1,0:T(8,128)(2,1)S(1)} %get-tuple-element.132), channel_id=1, source_target_pairs={{0,32},{8,40},{16,48},{24,56},{32,0},{40,8},{48,16},{56,24},{64,96... | collective-permute-start | bytes 442376 | tf_op jit(solution)/shard_map/ppermute | solution.py:56
  24.2 1.3 collective-permute-start.3
  25.5 2.5 %collective-permute-done.2 = bf16[72,1024]{1,0:T(8,128)(2,1)S(1)} collective-permute-done((bf16[72,1024]{1,0:T(8,128)(2,1)S(1)}, bf16[72,1024]{1,0:T(8,128)(2,1)S(1)}, u32[]{:S(2)}, u32[]{:S(2)}) %collective-permute-start.2) | collective-permute-done | bytes 147488 | tf_op jit(solution)/shard_map/ppermute | solution.py:56
  28.0 1.7 collective-permute-done.1
  31.6 3.1 %collective-permute-start.5 = (bf16[2,64,1024]{2,1,0:T(8,128)(2,1)S(1)}, bf16[2,64,1024]{2,1,0:T(8,128)(2,1)S(1)}, u32[]{:S(2)}, u32[]{:S(2)}) collective-permute-start(bf16[2,64,1024]{2,1,0:T(8,128)(2,1)S(1)} %pad_maximum_fusion.8), channel_id=1, source_target_pairs={{0,32},{8,40},{16,48},{24,56},{32,0},{40,8},{48,16},{56,24},{64,96... | collective-permute-start | bytes 786440 | tf_op jit(solution)/shard_map/ppermute | solution.py:56
  35.9 5.3 %collective-permute-done.6 = bf16[2,64,1024]{2,1,0:T(8,128)(2,1)S(1)} collective-permute-done((bf16[2,64,1024]{2,1,0:T(8,128)(2,1)S(1)}, bf16[2,64,1024]{2,1,0:T(8,128)(2,1)S(1)}, u32[]{:S(2)}, u32[]{:S(2)}) %collective-permute-start.6) | collective-permute-done | bytes 262176 | tf_op jit(solution)/shard_map/ppermute | solution.py:56
  41.2 3.9 %collective-permute-done.5 = bf16[2,64,1024]{2,1,0:T(8,128)(2,1)S(1)} collective-permute-done((bf16[2,64,1024]{2,1,0:T(8,128)(2,1)S(1)}, bf16[2,64,1024]{2,1,0:T(8,128)(2,1)S(1)}, u32[]{:S(2)}, u32[]{:S(2)}) %collective-permute-start.5) | collective-permute-done | bytes 262176 | tf_op jit(solution)/shard_map/ppermute | solution.py:56
  46.8 1.6 collective-permute-done.8.refs_2_.refs_3_.in1.up1
  48.4 1.0 copy-done.6
  49.4 6.6 %shard_map.111 = (bf16[4,2,64,1024]{3,2,1,0:T(8,128)(2,1)}, bf16[4,2,64,1024]{3,2,1,0:T(8,128)(2,1)}) custom-call(s32[3]{0:T(128)} %pad_add_fusion.at, bf16[8,72,1024]{2,1,0:T(8,128)(2,1)} %bitcast.170, bf16[8,72,1024]{2,1,0:T(8,128)(2,1)} %bitcast.171, bf16[8,72,1024]{2,1,0:T(8,128)(2,1)} %copy-done.6, bf16[8,72,1024]{2,1,0:T(8,128)(2,1)} %copy-done.6, ...), custom_call_target="tpu_custom_call" | custom-call | flops 2147483648 | bytes 8388608 | tf_op jit(solution)/shard_map/pallas_call | solution.py:189
  57.4 6.9 %shard_map.112 = (bf16[2,128,1024]{2,1,0:T(8,128)(2,1)}, bf16[2,128,1024]{2,1,0:T(8,128)(2,1)}, bf16[2,128,1024]{2,1,0:T(8,128)(2,1)}, bf16[2,128,1024]{2,1,0:T(8,128)(2,1)}) custom-call(s32[3]{0:T(128)} %pad_add_fusion.at, bf16[8,64,1024]{2,1,0:T(8,128)(2,1)} %bitcast.177, bf16[8,64,1024]{2,1,0:T(8,128)(2,1)} %bitcast.178, ...), custom_call_target="tpu_custom_call" | custom-call | flops 2147483648 | bytes 8388608 | tf_op jit(solution)/shard_map/pallas_call | solution.py:165
  64.2 2.1 collective-permute-start.11
  66.3 1.1 collective-permute-start.12
  67.5 1.4 collective-permute-start.13
  69.0 10.0 %collective-permute-done.11 = bf16[2,128,1024]{2,1,0:T(8,128)(2,1)S(1)} collective-permute-done((bf16[2,128,1024]{2,1,0:T(8,128)(2,1)}, bf16[2,128,1024]{2,1,0:T(8,128)(2,1)S(1)}, u32[]{:S(2)}, u32[]{:S(2)}) %collective-permute-start.11) | collective-permute-done | bytes 524320 | tf_op jit(solution)/shard_map/ppermute | solution.py:60
  79.0 11.6 %collective-permute-done.12 = bf16[2,128,1024]{2,1,0:T(8,128)(2,1)S(1)} collective-permute-done((bf16[2,128,1024]{2,1,0:T(8,128)(2,1)}, bf16[2,128,1024]{2,1,0:T(8,128)(2,1)S(1)}, u32[]{:S(2)}, u32[]{:S(2)}) %collective-permute-start.12) | collective-permute-done | bytes 524320 | tf_op jit(solution)/shard_map/ppermute | solution.py:60
  91.3 1.4 add_add_fusion
  93.1 1.6 collective-permute-start.14
  94.7 2.7 %collective-permute-start.15 = (bf16[2,64,1024]{2,1,0:T(8,128)(2,1)S(1)}, bf16[2,64,1024]{2,1,0:T(8,128)(2,1)S(1)}, u32[]{:S(2)}, u32[]{:S(2)}) collective-permute-start(bf16[2,64,1024]{2,1,0:T(8,128)(2,1)S(1)} %get-tuple-element.74), channel_id=1, source_target_pairs={{0,2},{1,3},{2,4},{3,5},{4,6},{5,7},{6,0},{7,1},{8,10},{9,11},{10,... | collective-permute-start | bytes 786440 | tf_op jit(solution)/shard_map/ppermute | solution.py:60
  97.5 1.9 collective-permute-start.17
  100.4 3.7 %collective-permute-done.15 = bf16[2,64,1024]{2,1,0:T(8,128)(2,1)S(1)} collective-permute-done((bf16[2,64,1024]{2,1,0:T(8,128)(2,1)S(1)}, bf16[2,64,1024]{2,1,0:T(8,128)(2,1)S(1)}, u32[]{:S(2)}, u32[]{:S(2)}) %collective-permute-start.15) | collective-permute-done | bytes 262176 | tf_op jit(solution)/shard_map/ppermute | solution.py:60
  104.1 5.0 %collective-permute-done.16 = bf16[2,64,1024]{2,1,0:T(8,128)(2,1)S(1)} collective-permute-done((bf16[2,64,1024]{2,1,0:T(8,128)(2,1)S(1)}, bf16[2,64,1024]{2,1,0:T(8,128)(2,1)S(1)}, u32[]{:S(2)}, u32[]{:S(2)}) %collective-permute-start.16) | collective-permute-done | bytes 262176 | tf_op jit(solution)/shard_map/ppermute | solution.py:60
  112.1 2.6 %collective-permute-start.21 = (bf16[2,64,1024]{2,1,0:T(8,128)(2,1)S(1)}, bf16[2,64,1024]{2,1,0:T(8,128)(2,1)S(1)}, u32[]{:S(2)}, u32[]{:S(2)}) collective-permute-start(bf16[2,64,1024]{2,1,0:T(8,128)(2,1)S(1)} %pad_maximum_fusion.11), channel_id=1, source_target_pairs={{0,2},{1,3},{2,4},{3,5},{4,6},{5,7},{6,0},{7,1},{8,10},{9,11},{10,... | collective-permute-start | bytes 786440 | tf_op jit(solution)/shard_map/ppermute | solution.py:60
  115.0 2.3 %collective-permute-start.19 = (bf16[2,64,1024]{2,1,0:T(8,128)(2,1)S(1)}, bf16[2,64,1024]{2,1,0:T(8,128)(2,1)S(1)}, u32[]{:S(2)}, u32[]{:S(2)}) collective-permute-start(bf16[2,64,1024]{2,1,0:T(8,128)(2,1)S(1)} %pad_maximum_fusion.11), channel_id=1, source_target_pairs={{0,6},{1,7},{2,0},{3,1},{4,2},{5,3},{6,4},{7,5},{8,14},{9,15},{10,... | collective-permute-start | bytes 786440 | tf_op jit(solution)/shard_map/ppermute | solution.py:60
  117.4 1.5 collective-permute-done.18
  118.8 2.7 %collective-permute-done.21 = bf16[2,64,1024]{2,1,0:T(8,128)(2,1)S(1)} collective-permute-done((bf16[2,64,1024]{2,1,0:T(8,128)(2,1)S(1)}, bf16[2,64,1024]{2,1,0:T(8,128)(2,1)S(1)}, u32[]{:S(2)}, u32[]{:S(2)}) %collective-permute-start.21) | collective-permute-done | bytes 262176 | tf_op jit(solution)/shard_map/ppermute | solution.py:60
  121.5 5.0 %collective-permute-done.20 = bf16[2,64,1024]{2,1,0:T(8,128)(2,1)S(1)} collective-permute-done((bf16[2,64,1024]{2,1,0:T(8,128)(2,1)S(1)}, bf16[2,64,1024]{2,1,0:T(8,128)(2,1)S(1)}, u32[]{:S(2)}, u32[]{:S(2)}) %collective-permute-start.20) | collective-permute-done | bytes 262176 | tf_op jit(solution)/shard_map/ppermute | solution.py:60
  129.0 1.1 pad_maximum_fusion.2.refs_0_.refs_2_
  130.1 1.5 collective-permute-start.25
  132.2 2.6 %collective-permute-start.24 = (bf16[2,128,1024]{2,1,0:T(8,128)(2,1)}, bf16[2,128,1024]{2,1,0:T(8,128)(2,1)}, u32[]{:S(2)}, u32[]{:S(2)}) collective-permute-start(bf16[2,128,1024]{2,1,0:T(8,128)(2,1)} %bitcast.183), channel_id=1, source_target_pairs={{0,2},{1,3},{2,4},{3,5},{4,6},{5,7},{6,0},{7,1},{8,10},{9,11},{10,... | collective-permute-start | bytes 1572872 | tf_op jit(solution)/shard_map/ppermute | solution.py:60
  135.6 2.6 %collective-permute-start.22 = (bf16[2,128,1024]{2,1,0:T(8,128)(2,1)}, bf16[2,128,1024]{2,1,0:T(8,128)(2,1)}, u32[]{:S(2)}, u32[]{:S(2)}) collective-permute-start(bf16[2,128,1024]{2,1,0:T(8,128)(2,1)} %bitcast.185), channel_id=1, source_target_pairs={{0,6},{1,7},{2,0},{3,1},{4,2},{5,3},{6,4},{7,5},{8,14},{9,15},{10,... | collective-permute-start | bytes 1572872 | tf_op jit(solution)/shard_map/ppermute | solution.py:60
  138.2 1.6 fusion.34
  140.1 8.0 %all-to-all-start.1 = ((f32[128,1,128]{2,1,0:T(1,128)}), f32[128,1,128]{2,1,0:T(1,128)S(1)}, u32[]{:S(2)}, u32[]{:S(2)}) async-start(f32[128,1,128]{2,1,0:T(1,128)} %broadcast_in_dim.152), calls=%async_computation.1 | async-start | bytes 131072 | tf_op jit(solution)/shard_map/all_to_all | solution.py:79
  148.2 13.4 %all-to-all-done.1 = f32[128,1,128]{2,1,0:T(1,128)S(1)} async-done(((f32[128,1,128]{2,1,0:T(1,128)}), f32[128,1,128]{2,1,0:T(1,128)S(1)}, u32[]{:S(2)}, u32[]{:S(2)}) %all-to-all-start.1) | async-done | bytes 65568 | tf_op jit(solution)/shard_map/all_to_all | solution.py:79
  164.4 4.0 %shard_map.113 = (f32[2,4,32,1024]{3,2,1,0:T(8,128)}, bf16[2,4,32,1024]{3,2,1,0:T(8,128)(2,1)}) custom-call(s32[3]{0:T(128)} %pad_add_fusion.at, bf16[2,128,1024]{2,1,0:T(8,128)(2,1)} %bitcast.186, bf16[2,128,1024]{2,1,0:T(8,128)(2,1)} %collective-permute-done.22.refs_1_.refs_5_, bf16[2,128,1024]{2,1,0:T(8,128)(2,1)} %collective-permute-done.23.refs_2_.refs_6_, ...), custom_call_target="tpu_custom_call" | custom-call | flops 1073741824 | bytes 4194304 | tf_op jit(solution)/shard_map/pallas_call | solution.py:236
  168.6 4.0 %shard_map.114 = (f32[2,4,32,1024]{3,2,1,0:T(8,128)}, bf16[2,4,32,1024]{3,2,1,0:T(8,128)(2,1)}) custom-call(s32[3]{0:T(128)} %pad_add_fusion.at, bf16[4,2,64,1024]{3,2,1,0:T(8,128)(2,1)} %pad_maximum_fusion.2.refs_0_.refs_2_, bf16[4,2,64,1024]{3,2,1,0:T(8,128)(2,1)} %collective-permute-done.25.refs_1_.refs_3_, bf16[2,1024,1024]{2,1,0:T(8,128)(2,1)} %refs_2_.1), custom_call_target="tpu_custom_call" | custom-call | flops 1073741824 | bytes 4194304 | tf_op jit(solution)/shard_map/pallas_call | solution.py:236
  175.1 1.1 pad_maximum_fusion.3
  176.2 4.2 %all-to-all-start.2 = ((bf16[8,2,32,1024]{3,2,1,0:T(8,128)(2,1)}), bf16[8,2,32,1024]{3,2,1,0:T(8,128)(2,1)S(1)}, u32[]{:S(2)}, u32[]{:S(2)}) async-start(bf16[8,2,32,1024]{3,2,1,0:T(8,128)(2,1)} %pad_maximum_fusion.3), calls=%async_computation.2 | async-start | bytes 2097152 | tf_op jit(solution)/shard_map/all_to_all | solution.py:51
  181.3 6.6 %shard_map.115 = (bf16[2,1024,1024]{2,1,0:T(8,128)(2,1)}, bf16[2,1024,1024]{2,1,0:T(8,128)(2,1)}) custom-call(s32[3]{0:T(128)} %pad_add_fusion.at, bf16[8,64,1024]{2,1,0:T(8,128)(2,1)} %bitcast.179, bf16[8,64,1024]{2,1,0:T(8,128)(2,1)} %bitcast.180, bf16[8,64,1024]{2,1,0:T(8,128)(2,1)} %collective-permute-done.9.refs_2_.refs_3_.in1.up1, ...), custom_call_target="tpu_custom_call" | custom-call | flops 2147483648 | bytes 8388608 | tf_op jit(solution)/shard_map/pallas_call | solution.py:274
  187.9 6.7 %shard_map.116 = (bf16[2,1024,1024]{2,1,0:T(8,128)(2,1)}, bf16[2,1024,1024]{2,1,0:T(8,128)(2,1)}) custom-call(s32[3]{0:T(128)} %pad_add_fusion.at, bf16[8,72,1024]{2,1,0:T(8,128)(2,1)} %bitcast.173, bf16[8,72,1024]{2,1,0:T(8,128)(2,1)} %bitcast.174, bf16[8,72,1024]{2,1,0:T(8,128)(2,1)} %copy-done.6, ...), custom_call_target="tpu_custom_call", output_to_operand_aliasing={{0}: (10, {}), {1}: (11, {})} | custom-call | flops 2147483648 | bytes 8388608 | tf_op jit(solution)/shard_map/pallas_call | solution.py:274
  194.6 1.6 all-to-all-done.2
  197.3 6.3 %all-to-all-start.3 = ((bf16[8,8,1024]{2,1,0:T(8,128)(2,1)}), bf16[8,8,1024]{2,1,0:T(8,128)(2,1)S(1)}, u32[]{:S(2)}, u32[]{:S(2)}) async-start(bf16[8,8,1024]{2,1,0:T(8,128)(2,1)} %copy.158), calls=%async_computation.3 | async-start | bytes 262144 | tf_op jit(solution)/shard_map/all_to_all | solution.py:422
  203.6 3.9 %collective-permute-start.28 = (f32[64,64]{1,0:T(8,128)S(1)}, f32[64,64]{1,0:T(8,128)S(1)}, u32[]{:S(2)}, u32[]{:S(2)}) collective-permute-start(f32[64,64]{1,0:T(8,128)S(1)} %convolution_add_fusion.1), channel_id=1, source_target_pairs={{0,0},{1,16},{2,32},{3,48},{4,64},{5,80},{6,96},{7,112},{8,1},{9,1... | collective-permute-start | bytes 49160 | tf_op jit(solution)/shard_map/ppermute | solution.py:457
  207.6 7.0 %collective-permute-done.28 = f32[64,64]{1,0:T(8,128)S(1)} collective-permute-done((f32[64,64]{1,0:T(8,128)S(1)}, f32[64,64]{1,0:T(8,128)S(1)}, u32[]{:S(2)}, u32[]{:S(2)}) %collective-permute-start.28) | collective-permute-done | bytes 16416 | tf_op jit(solution)/shard_map/ppermute | solution.py:457
  215.8 2.1 fusion
  (193 shorter events, 29.5 us)
Async XLA Ops:
  16.5 8.9 %collective-permute-start = (bf16[64,1024]{1,0:T(8,128)(2,1)S(1)}, bf16[64,1024]{1,0:T(8,128)(2,1)S(1)}, u32[]{:S(2)}, u32[]{:S(2)}) collective-permute-start(bf16[64,1024]{1,0:T(8,128)(2,1)S(1)} %slice.122), channel_id=1, source_target_pairs={{0,64},{8,72},{16,80},{24,88},{32,96},{40,104},{48,112},{56,120},{... | collective-permute-start | bytes 393224 | tf_op jit(solution)/shard_map/ppermute | solution.py:43
  19.5 8.5 %collective-permute-start.2 = (bf16[72,1024]{1,0:T(8,128)(2,1)S(1)}, bf16[72,1024]{1,0:T(8,128)(2,1)S(1)}, u32[]{:S(2)}, u32[]{:S(2)}) collective-permute-start(bf16[72,1024]{1,0:T(8,128)(2,1)S(1)} %get-tuple-element.132), channel_id=1, source_target_pairs={{0,32},{8,40},{16,48},{24,56},{32,0},{40,8},{48,16},{56,24},{64,96... | collective-permute-start | bytes 442376 | tf_op jit(solution)/shard_map/ppermute | solution.py:56
  23.4 6.3 %collective-permute-start.1 = (bf16[72,1024]{1,0:T(8,128)(2,1)S(1)}, bf16[72,1024]{1,0:T(8,128)(2,1)S(1)}, u32[]{:S(2)}, u32[]{:S(2)}) collective-permute-start(bf16[72,1024]{1,0:T(8,128)(2,1)S(1)} %get-tuple-element.132), channel_id=1, source_target_pairs={{0,48},{8,56},{16,0},{24,8},{32,16},{40,24},{48,32},{56,40},{64,11... | collective-permute-start | bytes 442376 | tf_op jit(solution)/shard_map/ppermute | solution.py:56
  24.2 6.4 %collective-permute-start.3 = (bf16[72,1024]{1,0:T(8,128)(2,1)S(1)}, bf16[72,1024]{1,0:T(8,128)(2,1)S(1)}, u32[]{:S(2)}, u32[]{:S(2)}) collective-permute-start(bf16[72,1024]{1,0:T(8,128)(2,1)S(1)} %get-tuple-element.132), channel_id=1, source_target_pairs={{0,16},{8,24},{16,32},{24,40},{32,48},{40,56},{48,0},{56,8},{64,80... | collective-permute-start | bytes 442376 | tf_op jit(solution)/shard_map/ppermute | solution.py:56
  30.6 14.6 %collective-permute-start.7 = (bf16[4,72,1024]{2,1,0:T(8,128)(2,1)S(1)}, bf16[4,72,1024]{2,1,0:T(8,128)(2,1)S(1)}, u32[]{:S(2)}, u32[]{:S(2)}) collective-permute-start(bf16[4,72,1024]{2,1,0:T(8,128)(2,1)S(1)} %pad_maximum_fusion.4), channel_id=1, source_target_pairs={{0,64},{8,72},{16,80},{24,88},{32,96},{40,104},{48,112},{56,120},{... | collective-permute-start | bytes 1769480 | tf_op jit(solution)/shard_map/ppermute | solution.py:43
  31.5 9.7 %collective-permute-start.6 = (bf16[2,64,1024]{2,1,0:T(8,128)(2,1)S(1)}, bf16[2,64,1024]{2,1,0:T(8,128)(2,1)S(1)}, u32[]{:S(2)}, u32[]{:S(2)}) collective-permute-start(bf16[2,64,1024]{2,1,0:T(8,128)(2,1)S(1)} %pad_maximum_fusion.8), channel_id=1, source_target_pairs={{0,16},{8,24},{16,32},{24,40},{32,48},{40,56},{48,0},{56,8},{64,80... | collective-permute-start | bytes 786440 | tf_op jit(solution)/shard_map/ppermute | solution.py:56
  31.6 13.4 %collective-permute-start.5 = (bf16[2,64,1024]{2,1,0:T(8,128)(2,1)S(1)}, bf16[2,64,1024]{2,1,0:T(8,128)(2,1)S(1)}, u32[]{:S(2)}, u32[]{:S(2)}) collective-permute-start(bf16[2,64,1024]{2,1,0:T(8,128)(2,1)S(1)} %pad_maximum_fusion.8), channel_id=1, source_target_pairs={{0,32},{8,40},{16,48},{24,56},{32,0},{40,8},{48,16},{56,24},{64,96... | collective-permute-start | bytes 786440 | tf_op jit(solution)/shard_map/ppermute | solution.py:56
  34.8 10.3 %collective-permute-start.4 = (bf16[2,64,1024]{2,1,0:T(8,128)(2,1)S(1)}, bf16[2,64,1024]{2,1,0:T(8,128)(2,1)S(1)}, u32[]{:S(2)}, u32[]{:S(2)}) collective-permute-start(bf16[2,64,1024]{2,1,0:T(8,128)(2,1)S(1)} %pad_maximum_fusion.8), channel_id=1, source_target_pairs={{0,48},{8,56},{16,0},{24,8},{32,16},{40,24},{48,32},{56,40},{64,11... | collective-permute-start | bytes 786440 | tf_op jit(solution)/shard_map/ppermute | solution.py:56
  45.4 2.9 %copy-start.2 = (bf16[2,4,72,1024]{3,2,1,0:T(8,128)(2,1)}, bf16[2,4,72,1024]{3,2,1,0:T(8,128)(2,1)S(1)}, u32[]{:S(2)}) copy-start(bf16[2,4,72,1024]{3,2,1,0:T(8,128)(2,1)S(1)} %pad_maximum_fusion) | copy-start | bytes 3538948
  45.5 2.9 %collective-permute-start.8 = (bf16[8,72,1024]{2,1,0:T(8,128)(2,1)S(1)}, bf16[8,72,1024]{2,1,0:T(8,128)(2,1)S(1)}, u32[]{:S(2)}, u32[]{:S(2)}) collective-permute-start(bf16[8,72,1024]{2,1,0:T(8,128)(2,1)S(1)} %bitcast.169), channel_id=1, source_target_pairs={{0,8},{8,0},{16,24},{24,16},{32,40},{40,32},{48,56},{56,48},{64,72... | collective-permute-start | bytes 3538952 | tf_op jit(solution)/shard_map/ppermute | solution.py:39
  46.2 11.2 %collective-permute-start.9 = (bf16[8,64,1024]{2,1,0:T(8,128)(2,1)S(1)}, bf16[8,64,1024]{2,1,0:T(8,128)(2,1)}, u32[]{:S(2)}, u32[]{:S(2)}) collective-permute-start(bf16[8,64,1024]{2,1,0:T(8,128)(2,1)S(1)} %bitcast.176), channel_id=1, source_target_pairs={{0,8},{8,0},{16,24},{24,16},{32,40},{40,32},{48,56},{56,48},{64,72... | collective-permute-start | bytes 3145736 | tf_op jit(solution)/shard_map/ppermute | solution.py:39
  56.0 35.3 %collective-permute-start.10 = (bf16[4,2,64,1024]{3,2,1,0:T(8,128)(2,1)}, bf16[4,2,64,1024]{3,2,1,0:T(8,128)(2,1)S(1)}, u32[]{:S(2)}, u32[]{:S(2)}) collective-permute-start(bf16[4,2,64,1024]{3,2,1,0:T(8,128)(2,1)} %get-tuple-element.62), channel_id=1, source_target_pairs={{0,1},{1,0},{2,3},{3,2},{4,5},{5,4},{6,7},{7,6},{8,9},{9,8},{10,11... | collective-permute-start | bytes 3145736 | tf_op jit(solution)/shard_map/ppermute | solution.py:47
  57.3 11.5 %copy-start.7 = (bf16[8,72,1024]{2,1,0:T(8,128)(2,1)S(1)}, bf16[8,72,1024]{2,1,0:T(8,128)(2,1)}, u32[]{:S(2)}) copy-start(bf16[8,72,1024]{2,1,0:T(8,128)(2,1)} %copy-done.6) | copy-start | bytes 3538948
  64.2 14.7 %collective-permute-start.11 = (bf16[2,128,1024]{2,1,0:T(8,128)(2,1)}, bf16[2,128,1024]{2,1,0:T(8,128)(2,1)S(1)}, u32[]{:S(2)}, u32[]{:S(2)}) collective-permute-start(bf16[2,128,1024]{2,1,0:T(8,128)(2,1)} %get-tuple-element.65), channel_id=1, source_target_pairs={{0,2},{1,3},{2,4},{3,5},{4,6},{5,7},{6,0},{7,1},{8,10},{9,11},{10,... | collective-permute-start | bytes 1572872 | tf_op jit(solution)/shard_map/ppermute | solution.py:60
  66.3 24.3 %collective-permute-start.12 = (bf16[2,128,1024]{2,1,0:T(8,128)(2,1)}, bf16[2,128,1024]{2,1,0:T(8,128)(2,1)S(1)}, u32[]{:S(2)}, u32[]{:S(2)}) collective-permute-start(bf16[2,128,1024]{2,1,0:T(8,128)(2,1)} %get-tuple-element.66), channel_id=1, source_target_pairs={{0,4},{1,5},{2,6},{3,7},{4,0},{5,1},{6,2},{7,3},{8,12},{9,13},{10,... | collective-permute-start | bytes 1572872 | tf_op jit(solution)/shard_map/ppermute | solution.py:60
  67.5 23.8 %collective-permute-start.13 = (bf16[2,128,1024]{2,1,0:T(8,128)(2,1)}, bf16[2,128,1024]{2,1,0:T(8,128)(2,1)S(1)}, u32[]{:S(2)}, u32[]{:S(2)}) collective-permute-start(bf16[2,128,1024]{2,1,0:T(8,128)(2,1)} %get-tuple-element.67), channel_id=1, source_target_pairs={{0,6},{1,7},{2,0},{3,1},{4,2},{5,3},{6,4},{7,5},{8,14},{9,15},{10,... | collective-permute-start | bytes 1572872 | tf_op jit(solution)/shard_map/ppermute | solution.py:60
  68.9 30.5 %copy-start.11 = (bf16[16,1,32,128]{3,2,1,0:T(8,128)(2,1)}, bf16[16,1,32,128]{3,2,1,0:T(8,128)(2,1)S(1)}, u32[]{:S(2)}) copy-start(bf16[16,1,32,128]{3,2,1,0:T(8,128)(2,1)S(1)} %get-tuple-element.125) | copy-start | bytes 393220
  69.0 23.8 %copy-start.15 = (bf16[4,2,64,1024]{3,2,1,0:T(8,128)(2,1)S(1)}, bf16[4,2,64,1024]{3,2,1,0:T(8,128)(2,1)}, u32[]{:S(2)}) copy-start(bf16[4,2,64,1024]{3,2,1,0:T(8,128)(2,1)} %get-tuple-element.71) | copy-start | bytes 3145732
  93.1 7.4 %collective-permute-start.14 = (bf16[2,64,1024]{2,1,0:T(8,128)(2,1)S(1)}, bf16[2,64,1024]{2,1,0:T(8,128)(2,1)S(1)}, u32[]{:S(2)}, u32[]{:S(2)}) collective-permute-start(bf16[2,64,1024]{2,1,0:T(8,128)(2,1)S(1)} %fusion.30), channel_id=1, source_target_pairs={{0,1},{1,0},{2,3},{3,2},{4,5},{5,4},{6,7},{7,6},{8,9},{9,8},{10,11... | collective-permute-start | bytes 786440 | tf_op jit(solution)/shard_map/ppermute | solution.py:47
  94.7 9.4 %collective-permute-start.15 = (bf16[2,64,1024]{2,1,0:T(8,128)(2,1)S(1)}, bf16[2,64,1024]{2,1,0:T(8,128)(2,1)S(1)}, u32[]{:S(2)}, u32[]{:S(2)}) collective-permute-start(bf16[2,64,1024]{2,1,0:T(8,128)(2,1)S(1)} %get-tuple-element.74), channel_id=1, source_target_pairs={{0,2},{1,3},{2,4},{3,5},{4,6},{5,7},{6,0},{7,1},{8,10},{9,11},{10,... | collective-permute-start | bytes 786440 | tf_op jit(solution)/shard_map/ppermute | solution.py:60
  97.4 11.7 %collective-permute-start.16 = (bf16[2,64,1024]{2,1,0:T(8,128)(2,1)S(1)}, bf16[2,64,1024]{2,1,0:T(8,128)(2,1)S(1)}, u32[]{:S(2)}, u32[]{:S(2)}) collective-permute-start(bf16[2,64,1024]{2,1,0:T(8,128)(2,1)S(1)} %get-tuple-element.75), channel_id=1, source_target_pairs={{0,4},{1,5},{2,6},{3,7},{4,0},{5,1},{6,2},{7,3},{8,12},{9,13},{10,... | collective-permute-start | bytes 786440 | tf_op jit(solution)/shard_map/ppermute | solution.py:60
  97.5 12.2 %collective-permute-start.17 = (bf16[2,64,1024]{2,1,0:T(8,128)(2,1)S(1)}, bf16[2,64,1024]{2,1,0:T(8,128)(2,1)S(1)}, u32[]{:S(2)}, u32[]{:S(2)}) collective-permute-start(bf16[2,64,1024]{2,1,0:T(8,128)(2,1)S(1)} %get-tuple-element.76), channel_id=1, source_target_pairs={{0,6},{1,7},{2,0},{3,1},{4,2},{5,3},{6,4},{7,5},{8,14},{9,15},{10,... | collective-permute-start | bytes 786440 | tf_op jit(solution)/shard_map/ppermute | solution.py:60
  99.5 9.6 %copy-start.10 = (f32[512,1]{1,0:T(8,128)}, f32[512,1]{1,0:T(8,128)S(1)}, u32[]{:S(2)}) copy-start(f32[512,1]{1,0:T(8,128)S(1)} %slice_convert_fusion.1.gate) | copy-start | bytes 6148
  99.6 9.5 %copy-start.9 = (f32[512,1]{1,0:T(8,128)}, f32[512,1]{1,0:T(8,128)S(1)}, u32[]{:S(2)}) copy-start(f32[512,1]{1,0:T(8,128)S(1)} %slice_convert_fusion.gate) | copy-start | bytes 6148
  111.6 7.2 %collective-permute-start.18 = (bf16[2,64,1024]{2,1,0:T(8,128)(2,1)S(1)}, bf16[2,64,1024]{2,1,0:T(8,128)(2,1)S(1)}, u32[]{:S(2)}, u32[]{:S(2)}) collective-permute-start(bf16[2,64,1024]{2,1,0:T(8,128)(2,1)S(1)} %pad_maximum_fusion.10), channel_id=1, source_target_pairs={{0,1},{1,0},{2,3},{3,2},{4,5},{5,4},{6,7},{7,6},{8,9},{9,8},{10,11... | collective-permute-start | bytes 786440 | tf_op jit(solution)/shard_map/ppermute | solution.py:47
  112.1 9.4 %collective-permute-start.21 = (bf16[2,64,1024]{2,1,0:T(8,128)(2,1)S(1)}, bf16[2,64,1024]{2,1,0:T(8,128)(2,1)S(1)}, u32[]{:S(2)}, u32[]{:S(2)}) collective-permute-start(bf16[2,64,1024]{2,1,0:T(8,128)(2,1)S(1)} %pad_maximum_fusion.11), channel_id=1, source_target_pairs={{0,2},{1,3},{2,4},{3,5},{4,6},{5,7},{6,0},{7,1},{8,10},{9,11},{10,... | collective-permute-start | bytes 786440 | tf_op jit(solution)/shard_map/ppermute | solution.py:60
  114.8 11.8 %collective-permute-start.20 = (bf16[2,64,1024]{2,1,0:T(8,128)(2,1)S(1)}, bf16[2,64,1024]{2,1,0:T(8,128)(2,1)S(1)}, u32[]{:S(2)}, u32[]{:S(2)}) collective-permute-start(bf16[2,64,1024]{2,1,0:T(8,128)(2,1)S(1)} %pad_maximum_fusion.11), channel_id=1, source_target_pairs={{0,4},{1,5},{2,6},{3,7},{4,0},{5,1},{6,2},{7,3},{8,12},{9,13},{10,... | collective-permute-start | bytes 786440 | tf_op jit(solution)/shard_map/ppermute | solution.py:60
  115.0 12.2 %collective-permute-start.19 = (bf16[2,64,1024]{2,1,0:T(8,128)(2,1)S(1)}, bf16[2,64,1024]{2,1,0:T(8,128)(2,1)S(1)}, u32[]{:S(2)}, u32[]{:S(2)}) collective-permute-start(bf16[2,64,1024]{2,1,0:T(8,128)(2,1)S(1)} %pad_maximum_fusion.11), channel_id=1, source_target_pairs={{0,6},{1,7},{2,0},{3,1},{4,2},{5,3},{6,4},{7,5},{8,14},{9,15},{10,... | collective-permute-start | bytes 786440 | tf_op jit(solution)/shard_map/ppermute | solution.py:60
  121.5 5.0 %copy-start.18 = (bf16[2,64,1024]{2,1,0:T(8,128)(2,1)}, bf16[2,64,1024]{2,1,0:T(8,128)(2,1)S(1)}, u32[]{:S(2)}) copy-start(bf16[2,64,1024]{2,1,0:T(8,128)(2,1)S(1)} %collective-permute-done.21) | copy-start | bytes 786436
  128.0 10.3 %copy-start.5 = (bf16[4,2,64,1024]{3,2,1,0:T(8,128)(2,1)S(1)}, bf16[4,2,64,1024]{3,2,1,0:T(8,128)(2,1)}, u32[]{:S(2)}) copy-start(bf16[4,2,64,1024]{3,2,1,0:T(8,128)(2,1)} %copy-done.4) | copy-start | bytes 3145732
  130.1 18.0 %copy-start.3 = (bf16[2,4,72,1024]{3,2,1,0:T(8,128)(2,1)S(1)}, bf16[2,4,72,1024]{3,2,1,0:T(8,128)(2,1)}, u32[]{:S(2)}) copy-start(bf16[2,4,72,1024]{3,2,1,0:T(8,128)(2,1)} %copy-done.2) | copy-start | bytes 3538948
  130.1 31.6 %collective-permute-start.25 = (bf16[4,2,64,1024]{3,2,1,0:T(8,128)(2,1)}, bf16[4,2,64,1024]{3,2,1,0:T(8,128)(2,1)}, u32[]{:S(2)}, u32[]{:S(2)}) collective-permute-start(bf16[4,2,64,1024]{3,2,1,0:T(8,128)(2,1)} %pad_maximum_fusion.2.refs_0_.refs_2_), channel_id=1, source_target_pairs={{0,1},{1,0},{2,3},{3,2},{4,5},{5,4},{6,7},{7,6},{8,9},{9,8},{10,11... | collective-permute-start | bytes 3145736 | tf_op jit(solution)/shard_map/ppermute | solution.py:47
  131.6 8.3 %copy-start.12 = (bf16[16,1,32,128]{3,2,1,0:T(8,128)(2,1)S(1)}, bf16[16,1,32,128]{3,2,1,0:T(8,128)(2,1)}, u32[]{:S(2)}) copy-start(bf16[16,1,32,128]{3,2,1,0:T(8,128)(2,1)} %copy-done.11) | copy-start | bytes 393220
  132.2 29.5 %collective-permute-start.24 = (bf16[2,128,1024]{2,1,0:T(8,128)(2,1)}, bf16[2,128,1024]{2,1,0:T(8,128)(2,1)}, u32[]{:S(2)}, u32[]{:S(2)}) collective-permute-start(bf16[2,128,1024]{2,1,0:T(8,128)(2,1)} %bitcast.183), channel_id=1, source_target_pairs={{0,2},{1,3},{2,4},{3,5},{4,6},{5,7},{6,0},{7,1},{8,10},{9,11},{10,... | collective-permute-start | bytes 1572872 | tf_op jit(solution)/shard_map/ppermute | solution.py:60
  134.8 26.8 %collective-permute-start.23 = (bf16[2,128,1024]{2,1,0:T(8,128)(2,1)}, bf16[2,128,1024]{2,1,0:T(8,128)(2,1)}, u32[]{:S(2)}, u32[]{:S(2)}) collective-permute-start(bf16[2,128,1024]{2,1,0:T(8,128)(2,1)} %bitcast.184), channel_id=1, source_target_pairs={{0,4},{1,5},{2,6},{3,7},{4,0},{5,1},{6,2},{7,3},{8,12},{9,13},{10,... | collective-permute-start | bytes 1572872 | tf_op jit(solution)/shard_map/ppermute | solution.py:60
  135.6 26.1 %collective-permute-start.22 = (bf16[2,128,1024]{2,1,0:T(8,128)(2,1)}, bf16[2,128,1024]{2,1,0:T(8,128)(2,1)}, u32[]{:S(2)}, u32[]{:S(2)}) collective-permute-start(bf16[2,128,1024]{2,1,0:T(8,128)(2,1)} %bitcast.185), channel_id=1, source_target_pairs={{0,6},{1,7},{2,0},{3,1},{4,2},{5,3},{6,4},{7,5},{8,14},{9,15},{10,... | collective-permute-start | bytes 1572872 | tf_op jit(solution)/shard_map/ppermute | solution.py:60
  140.1 21.5 %all-to-all-start.1 = ((f32[128,1,128]{2,1,0:T(1,128)}), f32[128,1,128]{2,1,0:T(1,128)S(1)}, u32[]{:S(2)}, u32[]{:S(2)}) async-start(f32[128,1,128]{2,1,0:T(1,128)} %broadcast_in_dim.152), calls=%async_computation.1 | async-start | bytes 131072 | tf_op jit(solution)/shard_map/all_to_all | solution.py:79
  168.4 5.6 %collective-permute-start.26 = (bf16[2,4,32,1024]{3,2,1,0:T(8,128)(2,1)}, bf16[2,4,32,1024]{3,2,1,0:T(8,128)(2,1)S(1)}, u32[]{:S(2)}, u32[]{:S(2)}) collective-permute-start(bf16[2,4,32,1024]{3,2,1,0:T(8,128)(2,1)} %get-tuple-element.98), channel_id=1, source_target_pairs={{0,8},{8,0},{16,24},{24,16},{32,40},{40,32},{48,56},{56,48},{64,72... | collective-permute-start | bytes 1572872 | tf_op jit(solution)/shard_map/ppermute | solution.py:39
  168.6 4.9 %copy-start.26 = (pred[64]{0:T(512)(128)(4,1)S(1)}, pred[64]{0:T(512)(128)(4,1)}, u32[]{:S(2)}) copy-start(pred[64]{0:T(512)(128)(4,1)} %get-tuple-element.144) | copy-start | bytes 196
  168.6 4.9 %copy-start.27 = (pred[64]{0:T(512)(128)(4,1)S(1)}, pred[64]{0:T(512)(128)(4,1)}, u32[]{:S(2)}) copy-start(pred[64]{0:T(512)(128)(4,1)} %get-tuple-element.143) | copy-start | bytes 196
  172.6 2.3 %collective-permute-start.27 = (bf16[2,4,32,1024]{3,2,1,0:T(8,128)(2,1)}, bf16[2,4,32,1024]{3,2,1,0:T(8,128)(2,1)S(1)}, u32[]{:S(2)}, u32[]{:S(2)}) collective-permute-start(bf16[2,4,32,1024]{3,2,1,0:T(8,128)(2,1)} %get-tuple-element.102), channel_id=1, source_target_pairs={{0,8},{8,0},{16,24},{24,16},{32,40},{40,32},{48,56},{56,48},{64,72... | collective-permute-start | bytes 1572872 | tf_op jit(solution)/shard_map/ppermute | solution.py:39
  175.1 5.4 %copy-start.24 = (bf16[2,8,32,64]{3,2,1,0:T(8,128)(2,1)S(1)}, bf16[2,8,32,64]{3,2,1,0:T(8,128)(2,1)}, u32[]{:S(2)}) copy-start(bf16[2,8,32,64]{3,2,1,0:T(8,128)(2,1)} %fusion.34) | copy-start | bytes 196612
  176.2 20.0 %all-to-all-start.2 = ((bf16[8,2,32,1024]{3,2,1,0:T(8,128)(2,1)}), bf16[8,2,32,1024]{3,2,1,0:T(8,128)(2,1)S(1)}, u32[]{:S(2)}, u32[]{:S(2)}) async-start(bf16[8,2,32,1024]{3,2,1,0:T(8,128)(2,1)} %pad_maximum_fusion.3), calls=%async_computation.2 | async-start | bytes 2097152 | tf_op jit(solution)/shard_map/all_to_all | solution.py:51
  194.6 9.0 %copy-start.25 = (s32[128,2]{0,1:T(2,128)S(1)}, s32[128,2]{0,1:T(2,128)}, u32[]{:S(2)}) copy-start(s32[128,2]{0,1:T(2,128)} %param.11) | copy-start | bytes 3076
  194.6 12.9 %copy-start.17 = (f32[128,64]{0,1:T(8,128)S(1)}, f32[128,64]{0,1:T(8,128)}, u32[]{:S(2)}) copy-start(f32[128,64]{0,1:T(8,128)} %param.10) | copy-start | bytes 98308
  197.3 17.3 %all-to-all-start.3 = ((bf16[8,8,1024]{2,1,0:T(8,128)(2,1)}), bf16[8,8,1024]{2,1,0:T(8,128)(2,1)S(1)}, u32[]{:S(2)}, u32[]{:S(2)}) async-start(bf16[8,8,1024]{2,1,0:T(8,128)(2,1)} %copy.158), calls=%async_computation.3 | async-start | bytes 262144 | tf_op jit(solution)/shard_map/all_to_all | solution.py:422
  203.6 10.9 %collective-permute-start.28 = (f32[64,64]{1,0:T(8,128)S(1)}, f32[64,64]{1,0:T(8,128)S(1)}, u32[]{:S(2)}, u32[]{:S(2)}) collective-permute-start(f32[64,64]{1,0:T(8,128)S(1)} %convolution_add_fusion.1), channel_id=1, source_target_pairs={{0,0},{1,16},{2,32},{3,48},{4,64},{5,80},{6,96},{7,112},{8,1},{9,1... | collective-permute-start | bytes 49160 | tf_op jit(solution)/shard_map/ppermute | solution.py:457
  214.6 3.9 %copy-start.1 = (bf16[128,8192]{1,0:T(8,128)(2,1)S(1)}, bf16[128,8192]{1,0:T(8,128)(2,1)}, u32[]{:S(2)}) copy-start(bf16[128,8192]{1,0:T(8,128)(2,1)} %param.9) | copy-start | bytes 6291460
  (12 other events, 16.2 us)

commit v2 on v1

--- a/solution.py
+++ b/solution.py
@@ -355,7 +355,7 @@
     kept1, sent1 = project_split(near[1], far[1], w_in, w_out, 1, spots)
     other1 = send_x(sent1)
     parts0 = project_whole(after(near[0], sent1), far[0], w_in, w_out, 0, spots)
-    got0 = [send_y(parts0[step], step) for step in range(1, 4)]
+    got0 = [send_y(parts0[step], step) for step in (2, 1, 3)]
     other1, got0 = together(other1, got0)
     half0 = (up(parts0[0]) + sum(up(part) for part in got0)).reshape(2, 2, 64, -1)
     half1 = [up(kept1[step]) + up(other1[step]) for step in range(4)]
@@ -382,12 +382,19 @@
         send_x(sent0), ring(sent1, send_y), score
     )
     pair0, ring1, score = together(
-        join_x(sent0, other0, x, 1).reshape(2, 128, -1), jnp.stack(ring1), score
-    )
+        join_x(sent0, other0, x, 1).reshape(2, 128, -1), ring1, score
+    )
+    ring1 = jnp.stack(ring1)
     *wide, score = together(
         ring(pair0, send_y), [ring1, send_x(ring1)], trade_all(score)
     )
-    score = jnp.sum(score.reshape(2, 4, 2, 8, flight, 2, span), axis=0)
+    back = []
+    for e in range(flight):
+        kept, sent = row_terms_of(wide[e], w_in, e, spots)
+        back.append(kept + up(send_core(sent)))
+    sent = jnp.stack(back, axis=2).astype(bf16).reshape(8, flight, span, feature_width)
+
+    score = jnp.sum(after(score, sent).reshape(2, 4, 2, 8, flight, 2, span), axis=0)
     score = jnp.stack(
         [
             score[:, :, :, 0].reshape(4, 2, 2, 4, 2, span),
@@ -406,21 +413,14 @@
         [score[:, 0, 0] + score[:, 1, 1], score[:, 0, 1] + score[:, 1, 0]], axis=1
     ).transpose(0, 1, 3, 2, 4)
 
-    back = []
-    for e in range(flight):
-        kept, sent = row_terms_of(wide[e], w_in, e, spots)
-        back.append(kept + up(send_core(sent)))
-    sent = jnp.stack(back, axis=2).astype(bf16).reshape(8, flight, span, feature_width)
     row_grads = jnp.sum(up(trade_places(sent)), axis=0).astype(bf16)
-    grads = ()
-    for e in range(flight):
-        grads = weight_grads(
-            near[e], far[e], after(gates[e], sent), wide[e], e, spots, grads
-        )
+    grads = weight_grads(near[0], far[0], after(gates[0], sent), wide[0], 0, spots)
+    row_grads = after(row_grads, grads[0])
+    grads = weight_grads(near[1], far[1], after(gates[1], row_grads), wide[1], 1, spots, grads)
     w_in_grad, w_out_grad = grads
 
     home = lax.all_to_all(
-        after(row_grads, w_in_grad).reshape(flight, 8, capacity, feature_width)
+        row_grads.reshape(flight, 8, capacity, feature_width)
         .transpose(1, 0, 2, 3)
         .reshape(8, flight * capacity, feature_width),
         "local",

time: 219 us -> 219 us (level)
    ppermute x1, waiting for transfers between devices: 7 us -> 0.01 us  [local(): lax.ppermute(router_terms, ('node', 'local'), [(i, i % 8 * 16 + i // 8) f...]
    ppermute x1, starting transfers between devices: 3.91 us -> 7.78 us  [local(): lax.ppermute(router_terms, ('node', 'local'), [(i, i % 8 * 16 + i // 8) f...]
    ppermute x6, waiting for transfers between devices: 14.2 us -> 17.6 us  [send_z(): return lax.ppermute(value, 'node', pairs)]
    ppermute x6, starting transfers between devices: 10.3 us -> 7.39 us  [send_z(): return lax.ppermute(value, 'node', pairs)]
    all_to_all x1, waiting for transfers between devices: 13.4 us -> 16.3 us  [trade_all(): return lax.all_to_all(value, ('node', 'local'), 0, 0, tiled=True)]
where the time goes in v2:
time: 219 us; the launch traced here: 216 us
  waiting for transfers between devices  80.1 us (37%)
  starting transfers between devices  61.3 us (28%)
  Pallas kernels  35.1 us (16%)
  other arithmetic  11.5 us (5%)
  blocking collectives  11 us (5%)
  local copies, waits for them, and re-layouts  10.2 us (5%)
  matrix products  5.56 us (3%)
    ppermute x12, waiting for transfers between devices, send_y(): lax.ppermute(value, 'local', [(i, (i // 2 + step) % 4 * 2 + i % 2) for i...  40.9 us
    ppermute x12, starting transfers between devices, send_y(): lax.ppermute(value, 'local', [(i, (i // 2 + step) % 4 * 2 + i % 2) for i...  19.3 us
    ppermute x6, waiting for transfers between devices, send_z(): return lax.ppermute(value, 'node', pairs)  17.6 us
    all_to_all x1, waiting for transfers between devices, trade_all(): return lax.all_to_all(value, ('node', 'local'), 0, 0, tiled=True)  16.3 us
    pallas_call x2, Pallas kernels, weight_grads(): call(kernel, (1024 // tile,), [scalar_spec] + row_specs() + [pl.BlockSpec...  13.3 us
    all_to_all x1, blocking collectives, local(): lax.all_to_all(jnp.concatenate([blocks, spread(facts, 8)], axis=2), 'loca...  11 us
    pallas_call x2, Pallas kernels, row_terms_of(): call(kernel, (1024 // wide,), [scalar_spec] + wide_specs(pieces, 1) + [pl...  8.4 us
    ppermute x1, starting transfers between devices, local(): lax.ppermute(router_terms, ('node', 'local'), [(i, i % 8 * 16 + i // 8) f...  7.78 us
  transfers between devices with their start and end apart: 32, of which 20 were waited for; matrix products, arithmetic and copies ran while one was open for 3% of the time, Pallas kernels for 14%

profile of v2, /device:TPU:16, one launch (start us, length us, event | category | flops | bytes accessed | tf_op | source)
XLA Modules:
  0.0 216.3 jit_solution(3600839498877618752)
XLA Ops:
  1.8 1.0 convolution_convert_fusion.2
  4.4 11.0 %all_to_all.20 = bf16[8,16,1152]{2,1,0:T(8,128)(2,1)S(1)} all-to-all(bf16[8,16,1152]{2,1,0:T(8,128)(2,1)S(1)} %pad_maximum_fusion.6), channel_id=1, replica_groups=mesh['node'=16,'local'=8] {'local'}, dimensions={0} | all-to-all | bytes 589824 | tf_op jit(solution)/shard_map/all_to_all | solution.py:318
  15.8 2.8 %collective-permute-start = (bf16[64,1024]{1,0:T(8,128)(2,1)S(1)}, bf16[64,1024]{1,0:T(8,128)(2,1)S(1)}, u32[]{:S(2)}, u32[]{:S(2)}) collective-permute-start(bf16[64,1024]{1,0:T(8,128)(2,1)S(1)} %slice.122), channel_id=1, source_target_pairs={{0,64},{8,72},{16,80},{24,88},{32,96},{40,104},{48,112},{56,120},{... | collective-permute-start | bytes 393224 | tf_op jit(solution)/shard_map/ppermute | solution.py:43
  18.8 4.1 %collective-permute-start.1 = (bf16[72,1024]{1,0:T(8,128)(2,1)S(1)}, bf16[72,1024]{1,0:T(8,128)(2,1)S(1)}, u32[]{:S(2)}, u32[]{:S(2)}) collective-permute-start(bf16[72,1024]{1,0:T(8,128)(2,1)S(1)} %get-tuple-element.140), channel_id=1, source_target_pairs={{0,48},{8,56},{16,0},{24,8},{32,16},{40,24},{48,32},{56,40},{64,11... | collective-permute-start | bytes 442376 | tf_op jit(solution)/shard_map/ppermute | solution.py:56
  22.9 1.3 collective-permute-start.3
  24.2 3.4 %collective-permute-done.1 = bf16[72,1024]{1,0:T(8,128)(2,1)S(1)} collective-permute-done((bf16[72,1024]{1,0:T(8,128)(2,1)S(1)}, bf16[72,1024]{1,0:T(8,128)(2,1)S(1)}, u32[]{:S(2)}, u32[]{:S(2)}) %collective-permute-start.1) | collective-permute-done | bytes 147488 | tf_op jit(solution)/shard_map/ppermute | solution.py:56
  27.6 2.3 %collective-permute-done.2 = bf16[72,1024]{1,0:T(8,128)(2,1)S(1)} collective-permute-done((bf16[72,1024]{1,0:T(8,128)(2,1)S(1)}, bf16[72,1024]{1,0:T(8,128)(2,1)S(1)}, u32[]{:S(2)}, u32[]{:S(2)}) %collective-permute-start.2) | collective-permute-done | bytes 147488 | tf_op jit(solution)/shard_map/ppermute | solution.py:56
  29.9 1.1 collective-permute-done.3
  34.1 5.8 %collective-permute-done.4 = bf16[2,64,1024]{2,1,0:T(8,128)(2,1)S(1)} collective-permute-done((bf16[2,64,1024]{2,1,0:T(8,128)(2,1)S(1)}, bf16[2,64,1024]{2,1,0:T(8,128)(2,1)S(1)}, u32[]{:S(2)}, u32[]{:S(2)}) %collective-permute-start.4) | collective-permute-done | bytes 262176 | tf_op jit(solution)/shard_map/ppermute | solution.py:56
  39.9 2.3 %collective-permute-done.5 = bf16[2,64,1024]{2,1,0:T(8,128)(2,1)S(1)} collective-permute-done((bf16[2,64,1024]{2,1,0:T(8,128)(2,1)S(1)}, bf16[2,64,1024]{2,1,0:T(8,128)(2,1)S(1)}, u32[]{:S(2)}, u32[]{:S(2)}) %collective-permute-start.5) | collective-permute-done | bytes 262176 | tf_op jit(solution)/shard_map/ppermute | solution.py:56
  42.2 2.7 %collective-permute-done.6 = bf16[2,64,1024]{2,1,0:T(8,128)(2,1)S(1)} collective-permute-done((bf16[2,64,1024]{2,1,0:T(8,128)(2,1)S(1)}, bf16[2,64,1024]{2,1,0:T(8,128)(2,1)S(1)}, u32[]{:S(2)}, u32[]{:S(2)}) %collective-permute-start.6) | collective-permute-done | bytes 262176 | tf_op jit(solution)/shard_map/ppermute | solution.py:56
  46.6 1.7 collective-permute-done.8.refs_2_.refs_3_.in1.up1
  48.2 1.0 copy-done.6
  49.3 6.6 %shard_map.111 = (bf16[4,2,64,1024]{3,2,1,0:T(8,128)(2,1)}, bf16[4,2,64,1024]{3,2,1,0:T(8,128)(2,1)}) custom-call(s32[3]{0:T(128)} %pad_add_fusion.at, bf16[8,72,1024]{2,1,0:T(8,128)(2,1)} %bitcast.170, bf16[8,72,1024]{2,1,0:T(8,128)(2,1)} %bitcast.171, bf16[8,72,1024]{2,1,0:T(8,128)(2,1)} %copy-done.6, bf16[8,72,1024]{2,1,0:T(8,128)(2,1)} %copy-done.6, ...), custom_call_target="tpu_custom_call" | custom-call | flops 2147483648 | bytes 8388608 | tf_op jit(solution)/shard_map/pallas_call | solution.py:189
  57.1 6.9 %shard_map.112 = (bf16[2,128,1024]{2,1,0:T(8,128)(2,1)}, bf16[2,128,1024]{2,1,0:T(8,128)(2,1)}, bf16[2,128,1024]{2,1,0:T(8,128)(2,1)}, bf16[2,128,1024]{2,1,0:T(8,128)(2,1)}) custom-call(s32[3]{0:T(128)} %pad_add_fusion.at, bf16[8,64,1024]{2,1,0:T(8,128)(2,1)} %bitcast.177, bf16[8,64,1024]{2,1,0:T(8,128)(2,1)} %bitcast.178, ...), custom_call_target="tpu_custom_call" | custom-call | flops 2147483648 | bytes 8388608 | tf_op jit(solution)/shard_map/pallas_call | solution.py:165
  64.0 2.1 collective-permute-start.11
  66.0 1.8 collective-permute-start.12
  68.3 12.3 %collective-permute-done.11 = bf16[2,128,1024]{2,1,0:T(8,128)(2,1)S(1)} collective-permute-done((bf16[2,128,1024]{2,1,0:T(8,128)(2,1)}, bf16[2,128,1024]{2,1,0:T(8,128)(2,1)S(1)}, u32[]{:S(2)}, u32[]{:S(2)}) %collective-permute-start.11) | collective-permute-done | bytes 524320 | tf_op jit(solution)/shard_map/ppermute | solution.py:60
  80.6 10.1 %collective-permute-done.12 = bf16[2,128,1024]{2,1,0:T(8,128)(2,1)S(1)} collective-permute-done((bf16[2,128,1024]{2,1,0:T(8,128)(2,1)}, bf16[2,128,1024]{2,1,0:T(8,128)(2,1)S(1)}, u32[]{:S(2)}, u32[]{:S(2)}) %collective-permute-start.12) | collective-permute-done | bytes 524320 | tf_op jit(solution)/shard_map/ppermute | solution.py:60
  91.8 1.3 collective-permute-start.14
  93.1 1.4 collective-permute-start.15
  95.4 2.1 collective-permute-start.17
  97.8 2.0 collective-permute-done.14
  99.8 2.0 collective-permute-done.15
  101.7 5.3 %collective-permute-done.16 = bf16[2,64,1024]{2,1,0:T(8,128)(2,1)S(1)} collective-permute-done((bf16[2,64,1024]{2,1,0:T(8,128)(2,1)S(1)}, bf16[2,64,1024]{2,1,0:T(8,128)(2,1)S(1)}, u32[]{:S(2)}, u32[]{:S(2)}) %collective-permute-start.16) | collective-permute-done | bytes 262176 | tf_op jit(solution)/shard_map/ppermute | solution.py:60
  107.0 1.4 collective-permute-done.17
  108.4 1.2 bitcast_add_fusion
  111.8 1.4 collective-permute-start.19
  113.2 3.2 %collective-permute-start.20 = (bf16[2,64,1024]{2,1,0:T(8,128)(2,1)S(1)}, bf16[2,64,1024]{2,1,0:T(8,128)(2,1)S(1)}, u32[]{:S(2)}, u32[]{:S(2)}) collective-permute-start(bf16[2,64,1024]{2,1,0:T(8,128)(2,1)S(1)} %pad_maximum_fusion.11), channel_id=1, source_target_pairs={{0,4},{1,5},{2,6},{3,7},{4,0},{5,1},{6,2},{7,3},{8,12},{9,13},{10,... | collective-permute-start | bytes 786440 | tf_op jit(solution)/shard_map/ppermute | solution.py:60
  116.9 1.5 collective-permute-done.18
  118.4 3.1 %collective-permute-done.19 = bf16[2,64,1024]{2,1,0:T(8,128)(2,1)S(1)} collective-permute-done((bf16[2,64,1024]{2,1,0:T(8,128)(2,1)S(1)}, bf16[2,64,1024]{2,1,0:T(8,128)(2,1)S(1)}, u32[]{:S(2)}, u32[]{:S(2)}) %collective-permute-start.19) | collective-permute-done | bytes 262176 | tf_op jit(solution)/shard_map/ppermute | solution.py:60
  121.5 2.5 %collective-permute-done.20 = bf16[2,64,1024]{2,1,0:T(8,128)(2,1)S(1)} collective-permute-done((bf16[2,64,1024]{2,1,0:T(8,128)(2,1)S(1)}, bf16[2,64,1024]{2,1,0:T(8,128)(2,1)S(1)}, u32[]{:S(2)}, u32[]{:S(2)}) %collective-permute-start.20) | collective-permute-done | bytes 262176 | tf_op jit(solution)/shard_map/ppermute | solution.py:60
  124.0 4.0 %collective-permute-done.21 = bf16[2,64,1024]{2,1,0:T(8,128)(2,1)S(1)} collective-permute-done((bf16[2,64,1024]{2,1,0:T(8,128)(2,1)S(1)}, bf16[2,64,1024]{2,1,0:T(8,128)(2,1)S(1)}, u32[]{:S(2)}, u32[]{:S(2)}) %collective-permute-start.21) | collective-permute-done | bytes 262176 | tf_op jit(solution)/shard_map/ppermute | solution.py:60
  129.1 1.5 collective-permute-start.25
  131.2 3.1 %collective-permute-start.23 = (bf16[2,128,1024]{2,1,0:T(8,128)(2,1)}, bf16[2,128,1024]{2,1,0:T(8,128)(2,1)}, u32[]{:S(2)}, u32[]{:S(2)}) collective-permute-start(bf16[2,128,1024]{2,1,0:T(8,128)(2,1)} %bitcast.53.refs_0_.refs_4_), channel_id=1, source_target_pairs={{0,4},{1,5},{2,6},{3,7},{4,0},{5,1},{6,2},{7,3},{8,12},{9,13},{10,... | collective-permute-start | bytes 1572872 | tf_op jit(solution)/shard_map/ppermute | solution.py:60
  134.4 1.8 collective-permute-start.24
  136.2 6.8 %all-to-all-start.1 = ((f32[128,1,128]{2,1,0:T(1,128)}), f32[128,1,128]{2,1,0:T(1,128)S(1)}, u32[]{:S(2)}, u32[]{:S(2)}) async-start(f32[128,1,128]{2,1,0:T(1,128)} %broadcast_in_dim.152), calls=%async_computation.1 | async-start | bytes 131072 | tf_op jit(solution)/shard_map/all_to_all | solution.py:79
  143.1 16.3 %all-to-all-done.1 = f32[128,1,128]{2,1,0:T(1,128)S(1)} async-done(((f32[128,1,128]{2,1,0:T(1,128)}), f32[128,1,128]{2,1,0:T(1,128)S(1)}, u32[]{:S(2)}, u32[]{:S(2)}) %all-to-all-start.1) | async-done | bytes 65568 | tf_op jit(solution)/shard_map/all_to_all | solution.py:79
  159.5 4.3 %shard_map.113 = (f32[2,4,32,1024]{3,2,1,0:T(8,128)}, bf16[2,4,32,1024]{3,2,1,0:T(8,128)(2,1)}) custom-call(s32[3]{0:T(128)} %pad_add_fusion.at, bf16[2,128,1024]{2,1,0:T(8,128)(2,1)} %bitcast.53.refs_0_.refs_4_, bf16[2,128,1024]{2,1,0:T(8,128)(2,1)} %collective-permute-done.22.refs_1_.refs_5_, ...), custom_call_target="tpu_custom_call" | custom-call | flops 1073741824 | bytes 4194304 | tf_op jit(solution)/shard_map/pallas_call | solution.py:236
  164.4 4.1 %shard_map.114 = (f32[2,4,32,1024]{3,2,1,0:T(8,128)}, bf16[2,4,32,1024]{3,2,1,0:T(8,128)(2,1)}) custom-call(s32[3]{0:T(128)} %pad_add_fusion.at, bf16[4,2,64,1024]{3,2,1,0:T(8,128)(2,1)} %copy-done.8, bf16[4,2,64,1024]{3,2,1,0:T(8,128)(2,1)} %copy-done.9, bf16[2,1024,1024]{2,1,0:T(8,128)(2,1)} %refs_2_.1), custom_call_target="tpu_custom_call" | custom-call | flops 1073741824 | bytes 4194304 | tf_op jit(solution)/shard_map/pallas_call | solution.py:236
  169.1 1.6 fusion.34
  172.4 1.1 pad_maximum_fusion.3
  175.8 5.0 %all-to-all-start.2 = ((bf16[8,2,32,1024]{3,2,1,0:T(8,128)(2,1)}), bf16[8,2,32,1024]{3,2,1,0:T(8,128)(2,1)S(1)}, u32[]{:S(2)}, u32[]{:S(2)}) async-start(bf16[8,2,32,1024]{3,2,1,0:T(8,128)(2,1)} %pad_maximum_fusion.3), calls=%async_computation.2 | async-start | bytes 2097152 | tf_op jit(solution)/shard_map/all_to_all | solution.py:51
  182.9 7.8 %collective-permute-start.28 = (f32[64,64]{1,0:T(8,128)S(1)}, f32[64,64]{1,0:T(8,128)S(1)}, u32[]{:S(2)}, u32[]{:S(2)}) collective-permute-start(f32[64,64]{1,0:T(8,128)S(1)} %convolution_add_fusion.1), channel_id=1, source_target_pairs={{0,0},{1,16},{2,32},{3,48},{4,64},{5,80},{6,96},{7,112},{8,1},{9,1... | collective-permute-start | bytes 49160 | tf_op jit(solution)/shard_map/ppermute | solution.py:457
  191.0 6.6 %shard_map.115 = (bf16[2,1024,1024]{2,1,0:T(8,128)(2,1)}, bf16[2,1024,1024]{2,1,0:T(8,128)(2,1)}) custom-call(s32[3]{0:T(128)} %pad_add_fusion.at, bf16[8,64,1024]{2,1,0:T(8,128)(2,1)} %bitcast.179, bf16[8,64,1024]{2,1,0:T(8,128)(2,1)} %bitcast.180, bf16[8,64,1024]{2,1,0:T(8,128)(2,1)} %collective-permute-done.9.refs_2_.refs_3_.in1.up1, ...), custom_call_target="tpu_custom_call" | custom-call | flops 2147483648 | bytes 8388608 | tf_op jit(solution)/shard_map/pallas_call | solution.py:274
  198.9 6.9 %all-to-all-start.3 = ((bf16[8,8,1024]{2,1,0:T(8,128)(2,1)}), bf16[8,8,1024]{2,1,0:T(8,128)(2,1)S(1)}, u32[]{:S(2)}, u32[]{:S(2)}) async-start(bf16[8,8,1024]{2,1,0:T(8,128)(2,1)} %copy.158), calls=%async_computation.3 | async-start | bytes 262144 | tf_op jit(solution)/shard_map/all_to_all | solution.py:422
  205.8 6.7 %shard_map.116 = (bf16[2,1024,1024]{2,1,0:T(8,128)(2,1)}, bf16[2,1024,1024]{2,1,0:T(8,128)(2,1)}) custom-call(s32[3]{0:T(128)} %pad_add_fusion.at, bf16[8,72,1024]{2,1,0:T(8,128)(2,1)} %bitcast.173, bf16[8,72,1024]{2,1,0:T(8,128)(2,1)} %bitcast.174, bf16[8,72,1024]{2,1,0:T(8,128)(2,1)} %copy-done.6, ...), custom_call_target="tpu_custom_call", output_to_operand_aliasing={{0}: (10, {}), {1}: (11, {})} | custom-call | flops 2147483648 | bytes 8388608 | tf_op jit(solution)/shard_map/pallas_call | solution.py:274
  213.7 2.1 fusion
  (193 shorter events, 26.6 us)
Async XLA Ops:
  15.8 8.3 %collective-permute-start = (bf16[64,1024]{1,0:T(8,128)(2,1)S(1)}, bf16[64,1024]{1,0:T(8,128)(2,1)S(1)}, u32[]{:S(2)}, u32[]{:S(2)}) collective-permute-start(bf16[64,1024]{1,0:T(8,128)(2,1)S(1)} %slice.122), channel_id=1, source_target_pairs={{0,64},{8,72},{16,80},{24,88},{32,96},{40,104},{48,112},{56,120},{... | collective-permute-start | bytes 393224 | tf_op jit(solution)/shard_map/ppermute | solution.py:43
  18.8 8.9 %collective-permute-start.1 = (bf16[72,1024]{1,0:T(8,128)(2,1)S(1)}, bf16[72,1024]{1,0:T(8,128)(2,1)S(1)}, u32[]{:S(2)}, u32[]{:S(2)}) collective-permute-start(bf16[72,1024]{1,0:T(8,128)(2,1)S(1)} %get-tuple-element.140), channel_id=1, source_target_pairs={{0,48},{8,56},{16,0},{24,8},{32,16},{40,24},{48,32},{56,40},{64,11... | collective-permute-start | bytes 442376 | tf_op jit(solution)/shard_map/ppermute | solution.py:56
  22.9 7.0 %collective-permute-start.2 = (bf16[72,1024]{1,0:T(8,128)(2,1)S(1)}, bf16[72,1024]{1,0:T(8,128)(2,1)S(1)}, u32[]{:S(2)}, u32[]{:S(2)}) collective-permute-start(bf16[72,1024]{1,0:T(8,128)(2,1)S(1)} %get-tuple-element.140), channel_id=1, source_target_pairs={{0,32},{8,40},{16,48},{24,56},{32,0},{40,8},{48,16},{56,24},{64,96... | collective-permute-start | bytes 442376 | tf_op jit(solution)/shard_map/ppermute | solution.py:56
  22.9 8.2 %collective-permute-start.3 = (bf16[72,1024]{1,0:T(8,128)(2,1)S(1)}, bf16[72,1024]{1,0:T(8,128)(2,1)S(1)}, u32[]{:S(2)}, u32[]{:S(2)}) collective-permute-start(bf16[72,1024]{1,0:T(8,128)(2,1)S(1)} %get-tuple-element.140), channel_id=1, source_target_pairs={{0,16},{8,24},{16,32},{24,40},{32,48},{40,56},{48,0},{56,8},{64,80... | collective-permute-start | bytes 442376 | tf_op jit(solution)/shard_map/ppermute | solution.py:56
  31.1 14.0 %collective-permute-start.7 = (bf16[4,72,1024]{2,1,0:T(8,128)(2,1)S(1)}, bf16[4,72,1024]{2,1,0:T(8,128)(2,1)S(1)}, u32[]{:S(2)}, u32[]{:S(2)}) collective-permute-start(bf16[4,72,1024]{2,1,0:T(8,128)(2,1)S(1)} %pad_maximum_fusion.4), channel_id=1, source_target_pairs={{0,64},{8,72},{16,80},{24,88},{32,96},{40,104},{48,112},{56,120},{... | collective-permute-start | bytes 1769480 | tf_op jit(solution)/shard_map/ppermute | solution.py:43
  32.0 7.9 %collective-permute-start.4 = (bf16[2,64,1024]{2,1,0:T(8,128)(2,1)S(1)}, bf16[2,64,1024]{2,1,0:T(8,128)(2,1)S(1)}, u32[]{:S(2)}, u32[]{:S(2)}) collective-permute-start(bf16[2,64,1024]{2,1,0:T(8,128)(2,1)S(1)} %pad_maximum_fusion.8), channel_id=1, source_target_pairs={{0,48},{8,56},{16,0},{24,8},{32,16},{40,24},{48,32},{56,40},{64,11... | collective-permute-start | bytes 786440 | tf_op jit(solution)/shard_map/ppermute | solution.py:56
  32.9 9.2 %collective-permute-start.5 = (bf16[2,64,1024]{2,1,0:T(8,128)(2,1)S(1)}, bf16[2,64,1024]{2,1,0:T(8,128)(2,1)S(1)}, u32[]{:S(2)}, u32[]{:S(2)}) collective-permute-start(bf16[2,64,1024]{2,1,0:T(8,128)(2,1)S(1)} %pad_maximum_fusion.8), channel_id=1, source_target_pairs={{0,32},{8,40},{16,48},{24,56},{32,0},{40,8},{48,16},{56,24},{64,96... | collective-permute-start | bytes 786440 | tf_op jit(solution)/shard_map/ppermute | solution.py:56
  33.1 11.7 %collective-permute-start.6 = (bf16[2,64,1024]{2,1,0:T(8,128)(2,1)S(1)}, bf16[2,64,1024]{2,1,0:T(8,128)(2,1)S(1)}, u32[]{:S(2)}, u32[]{:S(2)}) collective-permute-start(bf16[2,64,1024]{2,1,0:T(8,128)(2,1)S(1)} %pad_maximum_fusion.8), channel_id=1, source_target_pairs={{0,16},{8,24},{16,32},{24,40},{32,48},{40,56},{48,0},{56,8},{64,80... | collective-permute-start | bytes 786440 | tf_op jit(solution)/shard_map/ppermute | solution.py:56
  45.3 2.9 %collective-permute-start.8 = (bf16[8,72,1024]{2,1,0:T(8,128)(2,1)S(1)}, bf16[8,72,1024]{2,1,0:T(8,128)(2,1)S(1)}, u32[]{:S(2)}, u32[]{:S(2)}) collective-permute-start(bf16[8,72,1024]{2,1,0:T(8,128)(2,1)S(1)} %bitcast.169), channel_id=1, source_target_pairs={{0,8},{8,0},{16,24},{24,16},{32,40},{40,32},{48,56},{56,48},{64,72... | collective-permute-start | bytes 3538952 | tf_op jit(solution)/shard_map/ppermute | solution.py:39
  45.9 11.1 %collective-permute-start.9 = (bf16[8,64,1024]{2,1,0:T(8,128)(2,1)S(1)}, bf16[8,64,1024]{2,1,0:T(8,128)(2,1)}, u32[]{:S(2)}, u32[]{:S(2)}) collective-permute-start(bf16[8,64,1024]{2,1,0:T(8,128)(2,1)S(1)} %bitcast.176), channel_id=1, source_target_pairs={{0,8},{8,0},{16,24},{24,16},{32,40},{40,32},{48,56},{56,48},{64,72... | collective-permute-start | bytes 3145736 | tf_op jit(solution)/shard_map/ppermute | solution.py:39
  55.8 35.2 %collective-permute-start.10 = (bf16[4,2,64,1024]{3,2,1,0:T(8,128)(2,1)}, bf16[4,2,64,1024]{3,2,1,0:T(8,128)(2,1)S(1)}, u32[]{:S(2)}, u32[]{:S(2)}) collective-permute-start(bf16[4,2,64,1024]{3,2,1,0:T(8,128)(2,1)} %get-tuple-element.66), channel_id=1, source_target_pairs={{0,1},{1,0},{2,3},{3,2},{4,5},{5,4},{6,7},{7,6},{8,9},{9,8},{10,11... | collective-permute-start | bytes 3145736 | tf_op jit(solution)/shard_map/ppermute | solution.py:47
  57.1 11.2 %copy-start.7 = (bf16[8,72,1024]{2,1,0:T(8,128)(2,1)S(1)}, bf16[8,72,1024]{2,1,0:T(8,128)(2,1)}, u32[]{:S(2)}) copy-start(bf16[8,72,1024]{2,1,0:T(8,128)(2,1)} %copy-done.6) | copy-start | bytes 3538948
  64.0 27.1 %copy-start.17 = (bf16[4,2,64,1024]{3,2,1,0:T(8,128)(2,1)S(1)}, bf16[4,2,64,1024]{3,2,1,0:T(8,128)(2,1)}, u32[]{:S(2)}) copy-start(bf16[4,2,64,1024]{3,2,1,0:T(8,128)(2,1)} %get-tuple-element.75) | copy-start | bytes 3145732
  64.0 27.4 %copy-start.20 = (bf16[2,128,1024]{2,1,0:T(8,128)(2,1)S(1)}, bf16[2,128,1024]{2,1,0:T(8,128)(2,1)}, u32[]{:S(2)}) copy-start(bf16[2,128,1024]{2,1,0:T(8,128)(2,1)} %get-tuple-element.68) | copy-start | bytes 1572868
  64.0 16.6 %collective-permute-start.11 = (bf16[2,128,1024]{2,1,0:T(8,128)(2,1)}, bf16[2,128,1024]{2,1,0:T(8,128)(2,1)S(1)}, u32[]{:S(2)}, u32[]{:S(2)}) collective-permute-start(bf16[2,128,1024]{2,1,0:T(8,128)(2,1)} %get-tuple-element.69), channel_id=1, source_target_pairs={{0,4},{1,5},{2,6},{3,7},{4,0},{5,1},{6,2},{7,3},{8,12},{9,13},{10,... | collective-permute-start | bytes 1572872 | tf_op jit(solution)/shard_map/ppermute | solution.py:60
  66.0 24.7 %collective-permute-start.12 = (bf16[2,128,1024]{2,1,0:T(8,128)(2,1)}, bf16[2,128,1024]{2,1,0:T(8,128)(2,1)S(1)}, u32[]{:S(2)}, u32[]{:S(2)}) collective-permute-start(bf16[2,128,1024]{2,1,0:T(8,128)(2,1)} %get-tuple-element.70), channel_id=1, source_target_pairs={{0,2},{1,3},{2,4},{3,5},{4,6},{5,7},{6,0},{7,1},{8,10},{9,11},{10,... | collective-permute-start | bytes 1572872 | tf_op jit(solution)/shard_map/ppermute | solution.py:60
  67.9 23.2 %collective-permute-start.13 = (bf16[2,128,1024]{2,1,0:T(8,128)(2,1)}, bf16[2,128,1024]{2,1,0:T(8,128)(2,1)S(1)}, u32[]{:S(2)}, u32[]{:S(2)}) collective-permute-start(bf16[2,128,1024]{2,1,0:T(8,128)(2,1)} %get-tuple-element.71), channel_id=1, source_target_pairs={{0,6},{1,7},{2,0},{3,1},{4,2},{5,3},{6,4},{7,5},{8,14},{9,15},{10,... | collective-permute-start | bytes 1572872 | tf_op jit(solution)/shard_map/ppermute | solution.py:60
  68.3 29.2 %copy-start.13 = (bf16[16,1,32,128]{3,2,1,0:T(8,128)(2,1)}, bf16[16,1,32,128]{3,2,1,0:T(8,128)(2,1)S(1)}, u32[]{:S(2)}) copy-start(bf16[16,1,32,128]{3,2,1,0:T(8,128)(2,1)S(1)} %get-tuple-element.133) | copy-start | bytes 393220
  91.0 15.9 %copy-start.18 = (bf16[4,2,64,1024]{3,2,1,0:T(8,128)(2,1)}, bf16[4,2,64,1024]{3,2,1,0:T(8,128)(2,1)S(1)}, u32[]{:S(2)}) copy-start(bf16[4,2,64,1024]{3,2,1,0:T(8,128)(2,1)S(1)} %collective-permute-done.10) | copy-start | bytes 3145732
  91.8 8.0 %collective-permute-start.14 = (bf16[2,64,1024]{2,1,0:T(8,128)(2,1)S(1)}, bf16[2,64,1024]{2,1,0:T(8,128)(2,1)S(1)}, u32[]{:S(2)}, u32[]{:S(2)}) collective-permute-start(bf16[2,64,1024]{2,1,0:T(8,128)(2,1)S(1)} %fusion.30), channel_id=1, source_target_pairs={{0,1},{1,0},{2,3},{3,2},{4,5},{5,4},{6,7},{7,6},{8,9},{9,8},{10,11... | collective-permute-start | bytes 786440 | tf_op jit(solution)/shard_map/ppermute | solution.py:47
  93.1 8.6 %collective-permute-start.15 = (bf16[2,64,1024]{2,1,0:T(8,128)(2,1)S(1)}, bf16[2,64,1024]{2,1,0:T(8,128)(2,1)S(1)}, u32[]{:S(2)}, u32[]{:S(2)}) collective-permute-start(bf16[2,64,1024]{2,1,0:T(8,128)(2,1)S(1)} %get-tuple-element.78), channel_id=1, source_target_pairs={{0,2},{1,3},{2,4},{3,5},{4,6},{5,7},{6,0},{7,1},{8,10},{9,11},{10,... | collective-permute-start | bytes 786440 | tf_op jit(solution)/shard_map/ppermute | solution.py:60
  94.5 12.4 %collective-permute-start.16 = (bf16[2,64,1024]{2,1,0:T(8,128)(2,1)S(1)}, bf16[2,64,1024]{2,1,0:T(8,128)(2,1)S(1)}, u32[]{:S(2)}, u32[]{:S(2)}) collective-permute-start(bf16[2,64,1024]{2,1,0:T(8,128)(2,1)S(1)} %get-tuple-element.79), channel_id=1, source_target_pairs={{0,4},{1,5},{2,6},{3,7},{4,0},{5,1},{6,2},{7,3},{8,12},{9,13},{10,... | collective-permute-start | bytes 786440 | tf_op jit(solution)/shard_map/ppermute | solution.py:60
  95.4 12.9 %collective-permute-start.17 = (bf16[2,64,1024]{2,1,0:T(8,128)(2,1)S(1)}, bf16[2,64,1024]{2,1,0:T(8,128)(2,1)S(1)}, u32[]{:S(2)}, u32[]{:S(2)}) collective-permute-start(bf16[2,64,1024]{2,1,0:T(8,128)(2,1)S(1)} %get-tuple-element.80), channel_id=1, source_target_pairs={{0,6},{1,7},{2,0},{3,1},{4,2},{5,3},{6,4},{7,5},{8,14},{9,15},{10,... | collective-permute-start | bytes 786440 | tf_op jit(solution)/shard_map/ppermute | solution.py:60
  97.5 9.4 %copy-start.12 = (f32[512,1]{1,0:T(8,128)}, f32[512,1]{1,0:T(8,128)S(1)}, u32[]{:S(2)}) copy-start(f32[512,1]{1,0:T(8,128)S(1)} %slice_convert_fusion.1.gate) | copy-start | bytes 6148
  97.7 9.3 %copy-start.11 = (f32[512,1]{1,0:T(8,128)}, f32[512,1]{1,0:T(8,128)S(1)}, u32[]{:S(2)}) copy-start(f32[512,1]{1,0:T(8,128)S(1)} %slice_convert_fusion.gate) | copy-start | bytes 6148
  111.2 7.2 %collective-permute-start.18 = (bf16[2,64,1024]{2,1,0:T(8,128)(2,1)S(1)}, bf16[2,64,1024]{2,1,0:T(8,128)(2,1)S(1)}, u32[]{:S(2)}, u32[]{:S(2)}) collective-permute-start(bf16[2,64,1024]{2,1,0:T(8,128)(2,1)S(1)} %pad_maximum_fusion.10), channel_id=1, source_target_pairs={{0,1},{1,0},{2,3},{3,2},{4,5},{5,4},{6,7},{7,6},{8,9},{9,8},{10,11... | collective-permute-start | bytes 786440 | tf_op jit(solution)/shard_map/ppermute | solution.py:47
  111.8 9.7 %collective-permute-start.19 = (bf16[2,64,1024]{2,1,0:T(8,128)(2,1)S(1)}, bf16[2,64,1024]{2,1,0:T(8,128)(2,1)S(1)}, u32[]{:S(2)}, u32[]{:S(2)}) collective-permute-start(bf16[2,64,1024]{2,1,0:T(8,128)(2,1)S(1)} %pad_maximum_fusion.11), channel_id=1, source_target_pairs={{0,6},{1,7},{2,0},{3,1},{4,2},{5,3},{6,4},{7,5},{8,14},{9,15},{10,... | collective-permute-start | bytes 786440 | tf_op jit(solution)/shard_map/ppermute | solution.py:60
  113.2 10.8 %collective-permute-start.20 = (bf16[2,64,1024]{2,1,0:T(8,128)(2,1)S(1)}, bf16[2,64,1024]{2,1,0:T(8,128)(2,1)S(1)}, u32[]{:S(2)}, u32[]{:S(2)}) collective-permute-start(bf16[2,64,1024]{2,1,0:T(8,128)(2,1)S(1)} %pad_maximum_fusion.11), channel_id=1, source_target_pairs={{0,4},{1,5},{2,6},{3,7},{4,0},{5,1},{6,2},{7,3},{8,12},{9,13},{10,... | collective-permute-start | bytes 786440 | tf_op jit(solution)/shard_map/ppermute | solution.py:60
  116.4 11.6 %collective-permute-start.21 = (bf16[2,64,1024]{2,1,0:T(8,128)(2,1)S(1)}, bf16[2,64,1024]{2,1,0:T(8,128)(2,1)S(1)}, u32[]{:S(2)}, u32[]{:S(2)}) collective-permute-start(bf16[2,64,1024]{2,1,0:T(8,128)(2,1)S(1)} %pad_maximum_fusion.11), channel_id=1, source_target_pairs={{0,2},{1,3},{2,4},{3,5},{4,6},{5,7},{6,0},{7,1},{8,10},{9,11},{10,... | collective-permute-start | bytes 786440 | tf_op jit(solution)/shard_map/ppermute | solution.py:60
  129.1 34.6 %copy-start.8 = (bf16[4,2,64,1024]{3,2,1,0:T(8,128)(2,1)}, bf16[4,2,64,1024]{3,2,1,0:T(8,128)(2,1)S(1)}, u32[]{:S(2)}) copy-start(bf16[4,2,64,1024]{3,2,1,0:T(8,128)(2,1)S(1)} %pad_maximum_fusion.2.refs_0_.refs_2_) | copy-start | bytes 3145732
  129.1 30.3 %collective-permute-start.25 = (bf16[4,2,64,1024]{3,2,1,0:T(8,128)(2,1)S(1)}, bf16[4,2,64,1024]{3,2,1,0:T(8,128)(2,1)S(1)}, u32[]{:S(2)}, u32[]{:S(2)}) collective-permute-start(bf16[4,2,64,1024]{3,2,1,0:T(8,128)(2,1)S(1)} %pad_maximum_fusion.2.refs_0_.refs_2_), channel_id=1, source_target_pairs={{0,1},{1,0},{2,3},{3,2},{4,5},{5,4},{6,7},{7,6},{8,9},{9,8},{10,11... | collective-permute-start | bytes 3145736 | tf_op jit(solution)/shard_map/ppermute | solution.py:47
  130.6 28.8 %collective-permute-start.22 = (bf16[2,128,1024]{2,1,0:T(8,128)(2,1)}, bf16[2,128,1024]{2,1,0:T(8,128)(2,1)}, u32[]{:S(2)}, u32[]{:S(2)}) collective-permute-start(bf16[2,128,1024]{2,1,0:T(8,128)(2,1)} %bitcast.53.refs_0_.refs_4_), channel_id=1, source_target_pairs={{0,6},{1,7},{2,0},{3,1},{4,2},{5,3},{6,4},{7,5},{8,14},{9,15},{10,... | collective-permute-start | bytes 1572872 | tf_op jit(solution)/shard_map/ppermute | solution.py:60
  131.2 28.2 %collective-permute-start.23 = (bf16[2,128,1024]{2,1,0:T(8,128)(2,1)}, bf16[2,128,1024]{2,1,0:T(8,128)(2,1)}, u32[]{:S(2)}, u32[]{:S(2)}) collective-permute-start(bf16[2,128,1024]{2,1,0:T(8,128)(2,1)} %bitcast.53.refs_0_.refs_4_), channel_id=1, source_target_pairs={{0,4},{1,5},{2,6},{3,7},{4,0},{5,1},{6,2},{7,3},{8,12},{9,13},{10,... | collective-permute-start | bytes 1572872 | tf_op jit(solution)/shard_map/ppermute | solution.py:60
  134.4 25.0 %collective-permute-start.24 = (bf16[2,128,1024]{2,1,0:T(8,128)(2,1)}, bf16[2,128,1024]{2,1,0:T(8,128)(2,1)}, u32[]{:S(2)}, u32[]{:S(2)}) collective-permute-start(bf16[2,128,1024]{2,1,0:T(8,128)(2,1)} %bitcast.53.refs_0_.refs_4_), channel_id=1, source_target_pairs={{0,2},{1,3},{2,4},{3,5},{4,6},{5,7},{6,0},{7,1},{8,10},{9,11},{10,... | collective-permute-start | bytes 1572872 | tf_op jit(solution)/shard_map/ppermute | solution.py:60
  136.2 23.2 %all-to-all-start.1 = ((f32[128,1,128]{2,1,0:T(1,128)}), f32[128,1,128]{2,1,0:T(1,128)S(1)}, u32[]{:S(2)}, u32[]{:S(2)}) async-start(f32[128,1,128]{2,1,0:T(1,128)} %broadcast_in_dim.152), calls=%async_computation.1 | async-start | bytes 131072 | tf_op jit(solution)/shard_map/all_to_all | solution.py:79
  159.4 4.4 %copy-start.22 = (f32[128,1,128]{2,1,0:T(1,128)}, f32[128,1,128]{2,1,0:T(1,128)S(1)}, u32[]{:S(2)}) copy-start(f32[128,1,128]{2,1,0:T(1,128)S(1)} %all-to-all-done.1) | copy-start | bytes 196612
  159.4 4.3 %copy-start.9 = (bf16[4,2,64,1024]{3,2,1,0:T(8,128)(2,1)}, bf16[4,2,64,1024]{3,2,1,0:T(8,128)(2,1)S(1)}, u32[]{:S(2)}) copy-start(bf16[4,2,64,1024]{3,2,1,0:T(8,128)(2,1)S(1)} %collective-permute-done.25.refs_1_.refs_3_) | copy-start | bytes 3145732
  163.8 7.3 %collective-permute-start.26 = (bf16[2,4,32,1024]{3,2,1,0:T(8,128)(2,1)}, bf16[2,4,32,1024]{3,2,1,0:T(8,128)(2,1)S(1)}, u32[]{:S(2)}, u32[]{:S(2)}) collective-permute-start(bf16[2,4,32,1024]{3,2,1,0:T(8,128)(2,1)} %get-tuple-element.105), channel_id=1, source_target_pairs={{0,8},{8,0},{16,24},{24,16},{32,40},{40,32},{48,56},{56,48},{64,72... | collective-permute-start | bytes 1572872 | tf_op jit(solution)/shard_map/ppermute | solution.py:39
  164.4 4.6 %copy-start.5 = (bf16[4,2,64,1024]{3,2,1,0:T(8,128)(2,1)S(1)}, bf16[4,2,64,1024]{3,2,1,0:T(8,128)(2,1)}, u32[]{:S(2)}) copy-start(bf16[4,2,64,1024]{3,2,1,0:T(8,128)(2,1)} %copy-done.4) | copy-start | bytes 3145732
  168.5 3.5 %collective-permute-start.27 = (bf16[2,4,32,1024]{3,2,1,0:T(8,128)(2,1)}, bf16[2,4,32,1024]{3,2,1,0:T(8,128)(2,1)S(1)}, u32[]{:S(2)}, u32[]{:S(2)}) collective-permute-start(bf16[2,4,32,1024]{3,2,1,0:T(8,128)(2,1)} %get-tuple-element.109), channel_id=1, source_target_pairs={{0,8},{8,0},{16,24},{24,16},{32,40},{40,32},{48,56},{56,48},{64,72... | collective-permute-start | bytes 1572872 | tf_op jit(solution)/shard_map/ppermute | solution.py:39
  175.4 6.1 %copy-start.26 = (pred[64]{0:T(512)(128)(4,1)S(1)}, pred[64]{0:T(512)(128)(4,1)}, u32[]{:S(2)}) copy-start(pred[64]{0:T(512)(128)(4,1)} %get-tuple-element.152) | copy-start | bytes 196
  175.4 6.1 %copy-start.27 = (pred[64]{0:T(512)(128)(4,1)S(1)}, pred[64]{0:T(512)(128)(4,1)}, u32[]{:S(2)}) copy-start(pred[64]{0:T(512)(128)(4,1)} %get-tuple-element.151) | copy-start | bytes 196
  175.4 6.6 %copy-start.24 = (bf16[2,8,32,64]{3,2,1,0:T(8,128)(2,1)S(1)}, bf16[2,8,32,64]{3,2,1,0:T(8,128)(2,1)}, u32[]{:S(2)}) copy-start(bf16[2,8,32,64]{3,2,1,0:T(8,128)(2,1)} %fusion.34) | copy-start | bytes 196612
  175.8 15.2 %copy-start.25 = (s32[128,2]{0,1:T(2,128)S(1)}, s32[128,2]{0,1:T(2,128)}, u32[]{:S(2)}) copy-start(s32[128,2]{0,1:T(2,128)} %param.11) | copy-start | bytes 3076
  175.8 21.9 %all-to-all-start.2 = ((bf16[8,2,32,1024]{3,2,1,0:T(8,128)(2,1)}), bf16[8,2,32,1024]{3,2,1,0:T(8,128)(2,1)S(1)}, u32[]{:S(2)}, u32[]{:S(2)}) async-start(bf16[8,2,32,1024]{3,2,1,0:T(8,128)(2,1)} %pad_maximum_fusion.3), calls=%async_computation.2 | async-start | bytes 2097152 | tf_op jit(solution)/shard_map/all_to_all | solution.py:51
  182.9 14.8 %collective-permute-start.28 = (f32[64,64]{1,0:T(8,128)S(1)}, f32[64,64]{1,0:T(8,128)S(1)}, u32[]{:S(2)}, u32[]{:S(2)}) collective-permute-start(f32[64,64]{1,0:T(8,128)S(1)} %convolution_add_fusion.1), channel_id=1, source_target_pairs={{0,0},{1,16},{2,32},{3,48},{4,64},{5,80},{6,96},{7,112},{8,1},{9,1... | collective-permute-start | bytes 49160 | tf_op jit(solution)/shard_map/ppermute | solution.py:457
  191.0 6.7 %copy-start.21 = (f32[128,64]{0,1:T(8,128)S(1)}, f32[128,64]{0,1:T(8,128)}, u32[]{:S(2)}) copy-start(f32[128,64]{0,1:T(8,128)} %param.10) | copy-start | bytes 98308
  198.9 13.6 %all-to-all-start.3 = ((bf16[8,8,1024]{2,1,0:T(8,128)(2,1)}), bf16[8,8,1024]{2,1,0:T(8,128)(2,1)S(1)}, u32[]{:S(2)}, u32[]{:S(2)}) async-start(bf16[8,8,1024]{2,1,0:T(8,128)(2,1)} %copy.158), calls=%async_computation.3 | async-start | bytes 262144 | tf_op jit(solution)/shard_map/all_to_all | solution.py:422
  (12 other events, 22.9 us)

commit v3 on v1

--- a/solution.py
+++ b/solution.py
@@ -470,7 +470,7 @@
     logit_grad = (router_probs * centred).astype(bf16)
 
     combined = contract(placing, home, 0, 0)
-    router_part = contract(logit_grad, router_weight, 1, 1)
+    router_part = lax.optimization_barrier(contract(logit_grad, router_weight, 1, 1))
     token_grads = (combined + router_part).astype(bf16)
     return (token_grads, w_in_grad, w_out_grad, router_grad)
 

time: 219 us -> 224 us (1.023); the launches traced: 218 us -> 221 us
  waiting for transfers between devices: 80.1 us -> 71.9 us
  matrix products: 5.41 us -> 10.3 us
  starting transfers between devices: 61.6 us -> 66 us
    ppermute x1, waiting for transfers between devices: 7 us -> 0.01 us  [local(): lax.ppermute(router_terms, ('node', 'local'), [(i, i % 8 * 16 + i // 8) f...]
    dot_general x5, matrix products: 3.77 us -> 8.69 us  [contract(): lax.dot_general(left, right, (((left_dim,), (right_dim,)), ((), ())), pre...]
    ppermute x1, starting transfers between devices: 3.91 us -> 7.63 us  [local(): lax.ppermute(router_terms, ('node', 'local'), [(i, i % 8 * 16 + i // 8) f...]
    unnamed x60 -> x62, local copies, waits for them, and re-layouts: 5.74 us -> 5.3 us
  transfers between devices with their start and end apart: 32 -> 32, of which waited for: 20 -> 18; matrix products, arithmetic and copies ran while one was open for 3% -> 6% of each run, Pallas kernels for 14% -> 14%
where the time goes in v3:
time: 224 us; the launch traced here: 221 us
  waiting for transfers between devices  71.9 us (32%)
  starting transfers between devices  66 us (29%)
  Pallas kernels  34.7 us (15%)
  other arithmetic  14.2 us (6%)
  local copies, waits for them, and re-layouts  11.2 us (5%)
  blocking collectives  11 us (5%)
  matrix products  10.3 us (5%)
    ppermute x12, waiting for transfers between devices, send_y(): lax.ppermute(value, 'local', [(i, (i // 2 + step) % 4 * 2 + i % 2) for i...  39.4 us
    ppermute x12, starting transfers between devices, send_y(): lax.ppermute(value, 'local', [(i, (i // 2 + step) % 4 * 2 + i % 2) for i...  20.6 us
    ppermute x6, waiting for transfers between devices, send_z(): return lax.ppermute(value, 'node', pairs)  13.7 us
    all_to_all x1, waiting for transfers between devices, trade_all(): return lax.all_to_all(value, ('node', 'local'), 0, 0, tiled=True)  13.4 us
    pallas_call x2, Pallas kernels, weight_grads(): call(kernel, (1024 // tile,), [scalar_spec] + row_specs() + [pl.BlockSpec...  13.3 us
    all_to_all x1, blocking collectives, local(): lax.all_to_all(jnp.concatenate([blocks, spread(facts, 8)], axis=2), 'loca...  11 us
    ppermute x6, starting transfers between devices, send_z(): return lax.ppermute(value, 'node', pairs)  10.3 us
    dot_general x5, matrix products, contract(): lax.dot_general(left, right, (((left_dim,), (right_dim,)), ((), ())), pre...  8.69 us
  transfers between devices with their start and end apart: 32, of which 18 were waited for; matrix products, arithmetic and copies ran while one was open for 6% of the time, Pallas kernels for 14%

profile of v3, /device:TPU:16, one launch (start us, length us, event | category | flops | bytes accessed | tf_op | source)
XLA Modules:
  0.0 220.8 jit_solution(12169879282172989687)
XLA Ops:
  3.1 1.2 copy-done.8
  5.2 11.0 %all_to_all.20 = bf16[8,16,1152]{2,1,0:T(8,128)(2,1)S(1)} all-to-all(bf16[8,16,1152]{2,1,0:T(8,128)(2,1)S(1)} %pad_maximum_fusion.6), channel_id=1, replica_groups=mesh['node'=16,'local'=8] {'local'}, dimensions={0} | all-to-all | bytes 589824 | tf_op jit(solution)/shard_map/all_to_all | solution.py:318
  16.5 2.8 %collective-permute-start = (bf16[64,1024]{1,0:T(8,128)(2,1)S(1)}, bf16[64,1024]{1,0:T(8,128)(2,1)S(1)}, u32[]{:S(2)}, u32[]{:S(2)}) collective-permute-start(bf16[64,1024]{1,0:T(8,128)(2,1)S(1)} %slice.122), channel_id=1, source_target_pairs={{0,64},{8,72},{16,80},{24,88},{32,96},{40,104},{48,112},{56,120},{... | collective-permute-start | bytes 393224 | tf_op jit(solution)/shard_map/ppermute | solution.py:43
  19.5 4.0 %collective-permute-start.2 = (bf16[72,1024]{1,0:T(8,128)(2,1)S(1)}, bf16[72,1024]{1,0:T(8,128)(2,1)S(1)}, u32[]{:S(2)}, u32[]{:S(2)}) collective-permute-start(bf16[72,1024]{1,0:T(8,128)(2,1)S(1)} %get-tuple-element.132), channel_id=1, source_target_pairs={{0,32},{8,40},{16,48},{24,56},{32,0},{40,8},{48,16},{56,24},{64,96... | collective-permute-start | bytes 442376 | tf_op jit(solution)/shard_map/ppermute | solution.py:56
  24.2 1.3 collective-permute-start.3
  25.5 2.5 %collective-permute-done.2 = bf16[72,1024]{1,0:T(8,128)(2,1)S(1)} collective-permute-done((bf16[72,1024]{1,0:T(8,128)(2,1)S(1)}, bf16[72,1024]{1,0:T(8,128)(2,1)S(1)}, u32[]{:S(2)}, u32[]{:S(2)}) %collective-permute-start.2) | collective-permute-done | bytes 147488 | tf_op jit(solution)/shard_map/ppermute | solution.py:56
  28.0 1.7 collective-permute-done.1
  31.6 3.1 %collective-permute-start.5 = (bf16[2,64,1024]{2,1,0:T(8,128)(2,1)S(1)}, bf16[2,64,1024]{2,1,0:T(8,128)(2,1)S(1)}, u32[]{:S(2)}, u32[]{:S(2)}) collective-permute-start(bf16[2,64,1024]{2,1,0:T(8,128)(2,1)S(1)} %pad_maximum_fusion.8), channel_id=1, source_target_pairs={{0,32},{8,40},{16,48},{24,56},{32,0},{40,8},{48,16},{56,24},{64,96... | collective-permute-start | bytes 786440 | tf_op jit(solution)/shard_map/ppermute | solution.py:56
  36.4 4.8 %collective-permute-done.6 = bf16[2,64,1024]{2,1,0:T(8,128)(2,1)S(1)} collective-permute-done((bf16[2,64,1024]{2,1,0:T(8,128)(2,1)S(1)}, bf16[2,64,1024]{2,1,0:T(8,128)(2,1)S(1)}, u32[]{:S(2)}, u32[]{:S(2)}) %collective-permute-start.6) | collective-permute-done | bytes 262176 | tf_op jit(solution)/shard_map/ppermute | solution.py:56
  41.2 3.9 %collective-permute-done.5 = bf16[2,64,1024]{2,1,0:T(8,128)(2,1)S(1)} collective-permute-done((bf16[2,64,1024]{2,1,0:T(8,128)(2,1)S(1)}, bf16[2,64,1024]{2,1,0:T(8,128)(2,1)S(1)}, u32[]{:S(2)}, u32[]{:S(2)}) %collective-permute-start.5) | collective-permute-done | bytes 262176 | tf_op jit(solution)/shard_map/ppermute | solution.py:56
  46.8 1.6 collective-permute-done.8.refs_2_.refs_3_.in1.up1
  49.4 6.6 %shard_map.111 = (bf16[4,2,64,1024]{3,2,1,0:T(8,128)(2,1)}, bf16[4,2,64,1024]{3,2,1,0:T(8,128)(2,1)}) custom-call(s32[3]{0:T(128)} %pad_add_fusion.at, bf16[8,72,1024]{2,1,0:T(8,128)(2,1)} %bitcast.170, bf16[8,72,1024]{2,1,0:T(8,128)(2,1)} %bitcast.171, bf16[8,72,1024]{2,1,0:T(8,128)(2,1)} %copy-done.6, bf16[8,72,1024]{2,1,0:T(8,128)(2,1)} %copy-done.6, ...), custom_call_target="tpu_custom_call" | custom-call | flops 2147483648 | bytes 8388608 | tf_op jit(solution)/shard_map/pallas_call | solution.py:189
  57.4 6.9 %shard_map.112 = (bf16[2,128,1024]{2,1,0:T(8,128)(2,1)}, bf16[2,128,1024]{2,1,0:T(8,128)(2,1)}, bf16[2,128,1024]{2,1,0:T(8,128)(2,1)}, bf16[2,128,1024]{2,1,0:T(8,128)(2,1)}) custom-call(s32[3]{0:T(128)} %pad_add_fusion.at, bf16[8,64,1024]{2,1,0:T(8,128)(2,1)} %bitcast.177, bf16[8,64,1024]{2,1,0:T(8,128)(2,1)} %bitcast.178, ...), custom_call_target="tpu_custom_call" | custom-call | flops 2147483648 | bytes 8388608 | tf_op jit(solution)/shard_map/pallas_call | solution.py:165
  64.2 2.1 collective-permute-start.11
  66.3 1.2 collective-permute-start.12
  67.5 1.4 collective-permute-start.13
  69.0 10.0 %collective-permute-done.11 = bf16[2,128,1024]{2,1,0:T(8,128)(2,1)S(1)} collective-permute-done((bf16[2,128,1024]{2,1,0:T(8,128)(2,1)}, bf16[2,128,1024]{2,1,0:T(8,128)(2,1)S(1)}, u32[]{:S(2)}, u32[]{:S(2)}) %collective-permute-start.11) | collective-permute-done | bytes 524320 | tf_op jit(solution)/shard_map/ppermute | solution.py:60
  79.0 11.6 %collective-permute-done.12 = bf16[2,128,1024]{2,1,0:T(8,128)(2,1)S(1)} collective-permute-done((bf16[2,128,1024]{2,1,0:T(8,128)(2,1)}, bf16[2,128,1024]{2,1,0:T(8,128)(2,1)S(1)}, u32[]{:S(2)}, u32[]{:S(2)}) %collective-permute-start.12) | collective-permute-done | bytes 524320 | tf_op jit(solution)/shard_map/ppermute | solution.py:60
  91.3 1.4 add_add_fusion
  93.1 1.6 collective-permute-start.14
  94.7 2.7 %collective-permute-start.15 = (bf16[2,64,1024]{2,1,0:T(8,128)(2,1)S(1)}, bf16[2,64,1024]{2,1,0:T(8,128)(2,1)S(1)}, u32[]{:S(2)}, u32[]{:S(2)}) collective-permute-start(bf16[2,64,1024]{2,1,0:T(8,128)(2,1)S(1)} %get-tuple-element.74), channel_id=1, source_target_pairs={{0,2},{1,3},{2,4},{3,5},{4,6},{5,7},{6,0},{7,1},{8,10},{9,11},{10,... | collective-permute-start | bytes 786440 | tf_op jit(solution)/shard_map/ppermute | solution.py:60
  97.5 1.9 collective-permute-start.17
  100.4 3.7 %collective-permute-done.15 = bf16[2,64,1024]{2,1,0:T(8,128)(2,1)S(1)} collective-permute-done((bf16[2,64,1024]{2,1,0:T(8,128)(2,1)S(1)}, bf16[2,64,1024]{2,1,0:T(8,128)(2,1)S(1)}, u32[]{:S(2)}, u32[]{:S(2)}) %collective-permute-start.15) | collective-permute-done | bytes 262176 | tf_op jit(solution)/shard_map/ppermute | solution.py:60
  104.1 5.0 %collective-permute-done.16 = bf16[2,64,1024]{2,1,0:T(8,128)(2,1)S(1)} collective-permute-done((bf16[2,64,1024]{2,1,0:T(8,128)(2,1)S(1)}, bf16[2,64,1024]{2,1,0:T(8,128)(2,1)S(1)}, u32[]{:S(2)}, u32[]{:S(2)}) %collective-permute-start.16) | collective-permute-done | bytes 262176 | tf_op jit(solution)/shard_map/ppermute | solution.py:60
  112.2 2.6 %collective-permute-start.21 = (bf16[2,64,1024]{2,1,0:T(8,128)(2,1)S(1)}, bf16[2,64,1024]{2,1,0:T(8,128)(2,1)S(1)}, u32[]{:S(2)}, u32[]{:S(2)}) collective-permute-start(bf16[2,64,1024]{2,1,0:T(8,128)(2,1)S(1)} %pad_maximum_fusion.11), channel_id=1, source_target_pairs={{0,2},{1,3},{2,4},{3,5},{4,6},{5,7},{6,0},{7,1},{8,10},{9,11},{10,... | collective-permute-start | bytes 786440 | tf_op jit(solution)/shard_map/ppermute | solution.py:60
  115.0 2.3 %collective-permute-start.19 = (bf16[2,64,1024]{2,1,0:T(8,128)(2,1)S(1)}, bf16[2,64,1024]{2,1,0:T(8,128)(2,1)S(1)}, u32[]{:S(2)}, u32[]{:S(2)}) collective-permute-start(bf16[2,64,1024]{2,1,0:T(8,128)(2,1)S(1)} %pad_maximum_fusion.11), channel_id=1, source_target_pairs={{0,6},{1,7},{2,0},{3,1},{4,2},{5,3},{6,4},{7,5},{8,14},{9,15},{10,... | collective-permute-start | bytes 786440 | tf_op jit(solution)/shard_map/ppermute | solution.py:60
  117.4 1.5 collective-permute-done.18
  118.8 2.7 %collective-permute-done.21 = bf16[2,64,1024]{2,1,0:T(8,128)(2,1)S(1)} collective-permute-done((bf16[2,64,1024]{2,1,0:T(8,128)(2,1)S(1)}, bf16[2,64,1024]{2,1,0:T(8,128)(2,1)S(1)}, u32[]{:S(2)}, u32[]{:S(2)}) %collective-permute-start.21) | collective-permute-done | bytes 262176 | tf_op jit(solution)/shard_map/ppermute | solution.py:60
  121.5 5.0 %collective-permute-done.20 = bf16[2,64,1024]{2,1,0:T(8,128)(2,1)S(1)} collective-permute-done((bf16[2,64,1024]{2,1,0:T(8,128)(2,1)S(1)}, bf16[2,64,1024]{2,1,0:T(8,128)(2,1)S(1)}, u32[]{:S(2)}, u32[]{:S(2)}) %collective-permute-start.20) | collective-permute-done | bytes 262176 | tf_op jit(solution)/shard_map/ppermute | solution.py:60
  129.0 1.1 pad_maximum_fusion.2.refs_0_.refs_2_
  130.1 1.5 collective-permute-start.25
  132.2 2.6 %collective-permute-start.24 = (bf16[2,128,1024]{2,1,0:T(8,128)(2,1)}, bf16[2,128,1024]{2,1,0:T(8,128)(2,1)}, u32[]{:S(2)}, u32[]{:S(2)}) collective-permute-start(bf16[2,128,1024]{2,1,0:T(8,128)(2,1)} %bitcast.183), channel_id=1, source_target_pairs={{0,2},{1,3},{2,4},{3,5},{4,6},{5,7},{6,0},{7,1},{8,10},{9,11},{10,... | collective-permute-start | bytes 1572872 | tf_op jit(solution)/shard_map/ppermute | solution.py:60
  135.6 2.6 %collective-permute-start.22 = (bf16[2,128,1024]{2,1,0:T(8,128)(2,1)}, bf16[2,128,1024]{2,1,0:T(8,128)(2,1)}, u32[]{:S(2)}, u32[]{:S(2)}) collective-permute-start(bf16[2,128,1024]{2,1,0:T(8,128)(2,1)} %bitcast.185), channel_id=1, source_target_pairs={{0,6},{1,7},{2,0},{3,1},{4,2},{5,3},{6,4},{7,5},{8,14},{9,15},{10,... | collective-permute-start | bytes 1572872 | tf_op jit(solution)/shard_map/ppermute | solution.py:60
  138.3 1.6 fusion.34
  140.2 8.0 %all-to-all-start.1 = ((f32[128,1,128]{2,1,0:T(1,128)}), f32[128,1,128]{2,1,0:T(1,128)S(1)}, u32[]{:S(2)}, u32[]{:S(2)}) async-start(f32[128,1,128]{2,1,0:T(1,128)} %broadcast_in_dim.152), calls=%async_computation.1 | async-start | bytes 131072 | tf_op jit(solution)/shard_map/all_to_all | solution.py:79
  148.3 13.4 %all-to-all-done.1 = f32[128,1,128]{2,1,0:T(1,128)S(1)} async-done(((f32[128,1,128]{2,1,0:T(1,128)}), f32[128,1,128]{2,1,0:T(1,128)S(1)}, u32[]{:S(2)}, u32[]{:S(2)}) %all-to-all-start.1) | async-done | bytes 65568 | tf_op jit(solution)/shard_map/all_to_all | solution.py:79
  164.1 4.0 %shard_map.113 = (f32[2,4,32,1024]{3,2,1,0:T(8,128)}, bf16[2,4,32,1024]{3,2,1,0:T(8,128)(2,1)}) custom-call(s32[3]{0:T(128)} %pad_add_fusion.at, bf16[2,128,1024]{2,1,0:T(8,128)(2,1)} %bitcast.186, bf16[2,128,1024]{2,1,0:T(8,128)(2,1)} %collective-permute-done.22.refs_1_.refs_5_, bf16[2,128,1024]{2,1,0:T(8,128)(2,1)} %collective-permute-done.23.refs_2_.refs_6_, ...), custom_call_target="tpu_custom_call" | custom-call | flops 1073741824 | bytes 4194304 | tf_op jit(solution)/shard_map/pallas_call | solution.py:236
  168.2 4.0 %shard_map.114 = (f32[2,4,32,1024]{3,2,1,0:T(8,128)}, bf16[2,4,32,1024]{3,2,1,0:T(8,128)(2,1)}) custom-call(s32[3]{0:T(128)} %pad_add_fusion.at, bf16[4,2,64,1024]{3,2,1,0:T(8,128)(2,1)} %pad_maximum_fusion.2.refs_0_.refs_2_, bf16[4,2,64,1024]{3,2,1,0:T(8,128)(2,1)} %collective-permute-done.25.refs_1_.refs_3_, bf16[2,1024,1024]{2,1,0:T(8,128)(2,1)} %refs_2_.1), custom_call_target="tpu_custom_call" | custom-call | flops 1073741824 | bytes 4194304 | tf_op jit(solution)/shard_map/pallas_call | solution.py:236
  175.4 1.2 add_convert_fusion
  176.6 1.1 pad_maximum_fusion.3
  177.7 4.1 %all-to-all-start.2 = ((bf16[8,2,32,1024]{3,2,1,0:T(8,128)(2,1)}), bf16[8,2,32,1024]{3,2,1,0:T(8,128)(2,1)S(1)}, u32[]{:S(2)}, u32[]{:S(2)}) async-start(bf16[8,2,32,1024]{3,2,1,0:T(8,128)(2,1)} %pad_maximum_fusion.3), calls=%async_computation.2 | async-start | bytes 2097152 | tf_op jit(solution)/shard_map/all_to_all | solution.py:51
  182.3 7.6 %collective-permute-start.28 = (f32[64,64]{1,0:T(8,128)S(1)}, f32[64,64]{1,0:T(8,128)S(1)}, u32[]{:S(2)}, u32[]{:S(2)}) collective-permute-start(f32[64,64]{1,0:T(8,128)S(1)} %convolution_add_fusion.1), channel_id=1, source_target_pairs={{0,0},{1,16},{2,32},{3,48},{4,64},{5,80},{6,96},{7,112},{8,1},{9,1... | collective-permute-start | bytes 49160 | tf_op jit(solution)/shard_map/ppermute | solution.py:457
  190.0 6.6 %shard_map.115 = (bf16[2,1024,1024]{2,1,0:T(8,128)(2,1)}, bf16[2,1024,1024]{2,1,0:T(8,128)(2,1)}) custom-call(s32[3]{0:T(128)} %pad_add_fusion.at, bf16[8,64,1024]{2,1,0:T(8,128)(2,1)} %bitcast.179, bf16[8,64,1024]{2,1,0:T(8,128)(2,1)} %bitcast.180, bf16[8,64,1024]{2,1,0:T(8,128)(2,1)} %collective-permute-done.9.refs_2_.refs_3_.in1.up1, ...), custom_call_target="tpu_custom_call" | custom-call | flops 2147483648 | bytes 8388608 | tf_op jit(solution)/shard_map/pallas_call | solution.py:274
  196.7 6.7 %shard_map.116 = (bf16[2,1024,1024]{2,1,0:T(8,128)(2,1)}, bf16[2,1024,1024]{2,1,0:T(8,128)(2,1)}) custom-call(s32[3]{0:T(128)} %pad_add_fusion.at, bf16[8,72,1024]{2,1,0:T(8,128)(2,1)} %bitcast.173, bf16[8,72,1024]{2,1,0:T(8,128)(2,1)} %bitcast.174, bf16[8,72,1024]{2,1,0:T(8,128)(2,1)} %copy-done.6, ...), custom_call_target="tpu_custom_call", output_to_operand_aliasing={{0}: (10, {}), {1}: (11, {})} | custom-call | flops 2147483648 | bytes 8388608 | tf_op jit(solution)/shard_map/pallas_call | solution.py:274
  204.5 6.9 %all-to-all-start.3 = ((bf16[8,8,1024]{2,1,0:T(8,128)(2,1)}), bf16[8,8,1024]{2,1,0:T(8,128)(2,1)S(1)}, u32[]{:S(2)}, u32[]{:S(2)}) async-start(bf16[8,8,1024]{2,1,0:T(8,128)(2,1)} %copy.158), calls=%async_computation.3 | async-start | bytes 262144 | tf_op jit(solution)/shard_map/all_to_all | solution.py:422
  211.4 2.7 %fusion.49 = f32[128,8192]{1,0:T(8,128)} fusion(bf16[8192,64]{0,1:T(8,128)(2,1)S(1)} %copy-done.15, f32[128,64]{0,1:T(8,128)S(1)} %copy-done.17, f32[128,64]{0,1:T(8,128)S(1)} %select_reduce_fusion.2, f32[128]{0:T(128)S(1)} %multiply_reduce_fusion.2), kind=kOutput, calls=%fused_computation.124 | convolution fusion | flops 134242304 | bytes 5308928 | tf_op jit(solution)/shard_map/dot_general | solution.py:30
  214.1 1.7 all-to-all-done.3
  215.8 4.4 %fusion = bf16[128,8192]{1,0:T(8,128)(2,1)} fusion(f32[128,8192]{1,0:T(8,128)} %fusion.49, pred[8,128]{1,0:T(8,128)(4,1)S(1)} %fusion.59, bf16[8,8192]{1,0:T(8,128)(2,1)S(1)} %bitcast.205), kind=kOutput, calls=%fused_computation.1 | convolution fusion | flops 18874368 | bytes 6423552 | tf_op jit(solution)/shard_map/dot_general | solution.py:30
  (195 shorter events, 29.7 us)
Async XLA Ops:
  16.5 8.9 %collective-permute-start = (bf16[64,1024]{1,0:T(8,128)(2,1)S(1)}, bf16[64,1024]{1,0:T(8,128)(2,1)S(1)}, u32[]{:S(2)}, u32[]{:S(2)}) collective-permute-start(bf16[64,1024]{1,0:T(8,128)(2,1)S(1)} %slice.122), channel_id=1, source_target_pairs={{0,64},{8,72},{16,80},{24,88},{32,96},{40,104},{48,112},{56,120},{... | collective-permute-start | bytes 393224 | tf_op jit(solution)/shard_map/ppermute | solution.py:43
  19.5 8.5 %collective-permute-start.2 = (bf16[72,1024]{1,0:T(8,128)(2,1)S(1)}, bf16[72,1024]{1,0:T(8,128)(2,1)S(1)}, u32[]{:S(2)}, u32[]{:S(2)}) collective-permute-start(bf16[72,1024]{1,0:T(8,128)(2,1)S(1)} %get-tuple-element.132), channel_id=1, source_target_pairs={{0,32},{8,40},{16,48},{24,56},{32,0},{40,8},{48,16},{56,24},{64,96... | collective-permute-start | bytes 442376 | tf_op jit(solution)/shard_map/ppermute | solution.py:56
  23.4 6.3 %collective-permute-start.1 = (bf16[72,1024]{1,0:T(8,128)(2,1)S(1)}, bf16[72,1024]{1,0:T(8,128)(2,1)S(1)}, u32[]{:S(2)}, u32[]{:S(2)}) collective-permute-start(bf16[72,1024]{1,0:T(8,128)(2,1)S(1)} %get-tuple-element.132), channel_id=1, source_target_pairs={{0,48},{8,56},{16,0},{24,8},{32,16},{40,24},{48,32},{56,40},{64,11... | collective-permute-start | bytes 442376 | tf_op jit(solution)/shard_map/ppermute | solution.py:56
  24.2 6.4 %collective-permute-start.3 = (bf16[72,1024]{1,0:T(8,128)(2,1)S(1)}, bf16[72,1024]{1,0:T(8,128)(2,1)S(1)}, u32[]{:S(2)}, u32[]{:S(2)}) collective-permute-start(bf16[72,1024]{1,0:T(8,128)(2,1)S(1)} %get-tuple-element.132), channel_id=1, source_target_pairs={{0,16},{8,24},{16,32},{24,40},{32,48},{40,56},{48,0},{56,8},{64,80... | collective-permute-start | bytes 442376 | tf_op jit(solution)/shard_map/ppermute | solution.py:56
  30.6 14.6 %collective-permute-start.7 = (bf16[4,72,1024]{2,1,0:T(8,128)(2,1)S(1)}, bf16[4,72,1024]{2,1,0:T(8,128)(2,1)S(1)}, u32[]{:S(2)}, u32[]{:S(2)}) collective-permute-start(bf16[4,72,1024]{2,1,0:T(8,128)(2,1)S(1)} %pad_maximum_fusion.4), channel_id=1, source_target_pairs={{0,64},{8,72},{16,80},{24,88},{32,96},{40,104},{48,112},{56,120},{... | collective-permute-start | bytes 1769480 | tf_op jit(solution)/shard_map/ppermute | solution.py:43
  31.5 9.7 %collective-permute-start.6 = (bf16[2,64,1024]{2,1,0:T(8,128)(2,1)S(1)}, bf16[2,64,1024]{2,1,0:T(8,128)(2,1)S(1)}, u32[]{:S(2)}, u32[]{:S(2)}) collective-permute-start(bf16[2,64,1024]{2,1,0:T(8,128)(2,1)S(1)} %pad_maximum_fusion.8), channel_id=1, source_target_pairs={{0,16},{8,24},{16,32},{24,40},{32,48},{40,56},{48,0},{56,8},{64,80... | collective-permute-start | bytes 786440 | tf_op jit(solution)/shard_map/ppermute | solution.py:56
  31.6 13.4 %collective-permute-start.5 = (bf16[2,64,1024]{2,1,0:T(8,128)(2,1)S(1)}, bf16[2,64,1024]{2,1,0:T(8,128)(2,1)S(1)}, u32[]{:S(2)}, u32[]{:S(2)}) collective-permute-start(bf16[2,64,1024]{2,1,0:T(8,128)(2,1)S(1)} %pad_maximum_fusion.8), channel_id=1, source_target_pairs={{0,32},{8,40},{16,48},{24,56},{32,0},{40,8},{48,16},{56,24},{64,96... | collective-permute-start | bytes 786440 | tf_op jit(solution)/shard_map/ppermute | solution.py:56
  34.8 10.3 %collective-permute-start.4 = (bf16[2,64,1024]{2,1,0:T(8,128)(2,1)S(1)}, bf16[2,64,1024]{2,1,0:T(8,128)(2,1)S(1)}, u32[]{:S(2)}, u32[]{:S(2)}) collective-permute-start(bf16[2,64,1024]{2,1,0:T(8,128)(2,1)S(1)} %pad_maximum_fusion.8), channel_id=1, source_target_pairs={{0,48},{8,56},{16,0},{24,8},{32,16},{40,24},{48,32},{56,40},{64,11... | collective-permute-start | bytes 786440 | tf_op jit(solution)/shard_map/ppermute | solution.py:56
  45.5 2.9 %collective-permute-start.8 = (bf16[8,72,1024]{2,1,0:T(8,128)(2,1)S(1)}, bf16[8,72,1024]{2,1,0:T(8,128)(2,1)S(1)}, u32[]{:S(2)}, u32[]{:S(2)}) collective-permute-start(bf16[8,72,1024]{2,1,0:T(8,128)(2,1)S(1)} %bitcast.169), channel_id=1, source_target_pairs={{0,8},{8,0},{16,24},{24,16},{32,40},{40,32},{48,56},{56,48},{64,72... | collective-permute-start | bytes 3538952 | tf_op jit(solution)/shard_map/ppermute | solution.py:39
  46.2 11.2 %collective-permute-start.9 = (bf16[8,64,1024]{2,1,0:T(8,128)(2,1)S(1)}, bf16[8,64,1024]{2,1,0:T(8,128)(2,1)}, u32[]{:S(2)}, u32[]{:S(2)}) collective-permute-start(bf16[8,64,1024]{2,1,0:T(8,128)(2,1)S(1)} %bitcast.176), channel_id=1, source_target_pairs={{0,8},{8,0},{16,24},{24,16},{32,40},{40,32},{48,56},{56,48},{64,72... | collective-permute-start | bytes 3145736 | tf_op jit(solution)/shard_map/ppermute | solution.py:39
  56.0 35.3 %collective-permute-start.10 = (bf16[4,2,64,1024]{3,2,1,0:T(8,128)(2,1)}, bf16[4,2,64,1024]{3,2,1,0:T(8,128)(2,1)S(1)}, u32[]{:S(2)}, u32[]{:S(2)}) collective-permute-start(bf16[4,2,64,1024]{3,2,1,0:T(8,128)(2,1)} %get-tuple-element.62), channel_id=1, source_target_pairs={{0,1},{1,0},{2,3},{3,2},{4,5},{5,4},{6,7},{7,6},{8,9},{9,8},{10,11... | collective-permute-start | bytes 3145736 | tf_op jit(solution)/shard_map/ppermute | solution.py:47
  57.3 11.5 %copy-start.7 = (bf16[8,72,1024]{2,1,0:T(8,128)(2,1)S(1)}, bf16[8,72,1024]{2,1,0:T(8,128)(2,1)}, u32[]{:S(2)}) copy-start(bf16[8,72,1024]{2,1,0:T(8,128)(2,1)} %copy-done.6) | copy-start | bytes 3538948
  64.2 14.7 %collective-permute-start.11 = (bf16[2,128,1024]{2,1,0:T(8,128)(2,1)}, bf16[2,128,1024]{2,1,0:T(8,128)(2,1)S(1)}, u32[]{:S(2)}, u32[]{:S(2)}) collective-permute-start(bf16[2,128,1024]{2,1,0:T(8,128)(2,1)} %get-tuple-element.65), channel_id=1, source_target_pairs={{0,2},{1,3},{2,4},{3,5},{4,6},{5,7},{6,0},{7,1},{8,10},{9,11},{10,... | collective-permute-start | bytes 1572872 | tf_op jit(solution)/shard_map/ppermute | solution.py:60
  66.3 24.3 %collective-permute-start.12 = (bf16[2,128,1024]{2,1,0:T(8,128)(2,1)}, bf16[2,128,1024]{2,1,0:T(8,128)(2,1)S(1)}, u32[]{:S(2)}, u32[]{:S(2)}) collective-permute-start(bf16[2,128,1024]{2,1,0:T(8,128)(2,1)} %get-tuple-element.66), channel_id=1, source_target_pairs={{0,4},{1,5},{2,6},{3,7},{4,0},{5,1},{6,2},{7,3},{8,12},{9,13},{10,... | collective-permute-start | bytes 1572872 | tf_op jit(solution)/shard_map/ppermute | solution.py:60
  67.5 23.8 %collective-permute-start.13 = (bf16[2,128,1024]{2,1,0:T(8,128)(2,1)}, bf16[2,128,1024]{2,1,0:T(8,128)(2,1)S(1)}, u32[]{:S(2)}, u32[]{:S(2)}) collective-permute-start(bf16[2,128,1024]{2,1,0:T(8,128)(2,1)} %get-tuple-element.67), channel_id=1, source_target_pairs={{0,6},{1,7},{2,0},{3,1},{4,2},{5,3},{6,4},{7,5},{8,14},{9,15},{10,... | collective-permute-start | bytes 1572872 | tf_op jit(solution)/shard_map/ppermute | solution.py:60
  68.9 30.5 %copy-start.11 = (bf16[16,1,32,128]{3,2,1,0:T(8,128)(2,1)}, bf16[16,1,32,128]{3,2,1,0:T(8,128)(2,1)S(1)}, u32[]{:S(2)}) copy-start(bf16[16,1,32,128]{3,2,1,0:T(8,128)(2,1)S(1)} %get-tuple-element.125) | copy-start | bytes 393220
  69.0 23.8 %copy-start.16 = (bf16[4,2,64,1024]{3,2,1,0:T(8,128)(2,1)S(1)}, bf16[4,2,64,1024]{3,2,1,0:T(8,128)(2,1)}, u32[]{:S(2)}) copy-start(bf16[4,2,64,1024]{3,2,1,0:T(8,128)(2,1)} %get-tuple-element.71) | copy-start | bytes 3145732
  93.1 7.4 %collective-permute-start.14 = (bf16[2,64,1024]{2,1,0:T(8,128)(2,1)S(1)}, bf16[2,64,1024]{2,1,0:T(8,128)(2,1)S(1)}, u32[]{:S(2)}, u32[]{:S(2)}) collective-permute-start(bf16[2,64,1024]{2,1,0:T(8,128)(2,1)S(1)} %fusion.30), channel_id=1, source_target_pairs={{0,1},{1,0},{2,3},{3,2},{4,5},{5,4},{6,7},{7,6},{8,9},{9,8},{10,11... | collective-permute-start | bytes 786440 | tf_op jit(solution)/shard_map/ppermute | solution.py:47
  94.7 9.4 %collective-permute-start.15 = (bf16[2,64,1024]{2,1,0:T(8,128)(2,1)S(1)}, bf16[2,64,1024]{2,1,0:T(8,128)(2,1)S(1)}, u32[]{:S(2)}, u32[]{:S(2)}) collective-permute-start(bf16[2,64,1024]{2,1,0:T(8,128)(2,1)S(1)} %get-tuple-element.74), channel_id=1, source_target_pairs={{0,2},{1,3},{2,4},{3,5},{4,6},{5,7},{6,0},{7,1},{8,10},{9,11},{10,... | collective-permute-start | bytes 786440 | tf_op jit(solution)/shard_map/ppermute | solution.py:60
  97.4 11.7 %collective-permute-start.16 = (bf16[2,64,1024]{2,1,0:T(8,128)(2,1)S(1)}, bf16[2,64,1024]{2,1,0:T(8,128)(2,1)S(1)}, u32[]{:S(2)}, u32[]{:S(2)}) collective-permute-start(bf16[2,64,1024]{2,1,0:T(8,128)(2,1)S(1)} %get-tuple-element.75), channel_id=1, source_target_pairs={{0,4},{1,5},{2,6},{3,7},{4,0},{5,1},{6,2},{7,3},{8,12},{9,13},{10,... | collective-permute-start | bytes 786440 | tf_op jit(solution)/shard_map/ppermute | solution.py:60
  97.5 12.2 %collective-permute-start.17 = (bf16[2,64,1024]{2,1,0:T(8,128)(2,1)S(1)}, bf16[2,64,1024]{2,1,0:T(8,128)(2,1)S(1)}, u32[]{:S(2)}, u32[]{:S(2)}) collective-permute-start(bf16[2,64,1024]{2,1,0:T(8,128)(2,1)S(1)} %get-tuple-element.76), channel_id=1, source_target_pairs={{0,6},{1,7},{2,0},{3,1},{4,2},{5,3},{6,4},{7,5},{8,14},{9,15},{10,... | collective-permute-start | bytes 786440 | tf_op jit(solution)/shard_map/ppermute | solution.py:60
  99.5 9.6 %copy-start.10 = (f32[512,1]{1,0:T(8,128)}, f32[512,1]{1,0:T(8,128)S(1)}, u32[]{:S(2)}) copy-start(f32[512,1]{1,0:T(8,128)S(1)} %slice_convert_fusion.1.gate) | copy-start | bytes 6148
  99.6 9.5 %copy-start.9 = (f32[512,1]{1,0:T(8,128)}, f32[512,1]{1,0:T(8,128)S(1)}, u32[]{:S(2)}) copy-start(f32[512,1]{1,0:T(8,128)S(1)} %slice_convert_fusion.gate) | copy-start | bytes 6148
  111.7 7.2 %collective-permute-start.18 = (bf16[2,64,1024]{2,1,0:T(8,128)(2,1)S(1)}, bf16[2,64,1024]{2,1,0:T(8,128)(2,1)S(1)}, u32[]{:S(2)}, u32[]{:S(2)}) collective-permute-start(bf16[2,64,1024]{2,1,0:T(8,128)(2,1)S(1)} %pad_maximum_fusion.10), channel_id=1, source_target_pairs={{0,1},{1,0},{2,3},{3,2},{4,5},{5,4},{6,7},{7,6},{8,9},{9,8},{10,11... | collective-permute-start | bytes 786440 | tf_op jit(solution)/shard_map/ppermute | solution.py:47
  112.2 9.4 %collective-permute-start.21 = (bf16[2,64,1024]{2,1,0:T(8,128)(2,1)S(1)}, bf16[2,64,1024]{2,1,0:T(8,128)(2,1)S(1)}, u32[]{:S(2)}, u32[]{:S(2)}) collective-permute-start(bf16[2,64,1024]{2,1,0:T(8,128)(2,1)S(1)} %pad_maximum_fusion.11), channel_id=1, source_target_pairs={{0,2},{1,3},{2,4},{3,5},{4,6},{5,7},{6,0},{7,1},{8,10},{9,11},{10,... | collective-permute-start | bytes 786440 | tf_op jit(solution)/shard_map/ppermute | solution.py:60
  114.8 11.8 %collective-permute-start.20 = (bf16[2,64,1024]{2,1,0:T(8,128)(2,1)S(1)}, bf16[2,64,1024]{2,1,0:T(8,128)(2,1)S(1)}, u32[]{:S(2)}, u32[]{:S(2)}) collective-permute-start(bf16[2,64,1024]{2,1,0:T(8,128)(2,1)S(1)} %pad_maximum_fusion.11), channel_id=1, source_target_pairs={{0,4},{1,5},{2,6},{3,7},{4,0},{5,1},{6,2},{7,3},{8,12},{9,13},{10,... | collective-permute-start | bytes 786440 | tf_op jit(solution)/shard_map/ppermute | solution.py:60
  115.0 12.2 %collective-permute-start.19 = (bf16[2,64,1024]{2,1,0:T(8,128)(2,1)S(1)}, bf16[2,64,1024]{2,1,0:T(8,128)(2,1)S(1)}, u32[]{:S(2)}, u32[]{:S(2)}) collective-permute-start(bf16[2,64,1024]{2,1,0:T(8,128)(2,1)S(1)} %pad_maximum_fusion.11), channel_id=1, source_target_pairs={{0,6},{1,7},{2,0},{3,1},{4,2},{5,3},{6,4},{7,5},{8,14},{9,15},{10,... | collective-permute-start | bytes 786440 | tf_op jit(solution)/shard_map/ppermute | solution.py:60
  121.5 5.1 %copy-start.18 = (bf16[2,64,1024]{2,1,0:T(8,128)(2,1)}, bf16[2,64,1024]{2,1,0:T(8,128)(2,1)S(1)}, u32[]{:S(2)}) copy-start(bf16[2,64,1024]{2,1,0:T(8,128)(2,1)S(1)} %collective-permute-done.21) | copy-start | bytes 786436
  128.0 10.3 %copy-start.5 = (bf16[4,2,64,1024]{3,2,1,0:T(8,128)(2,1)S(1)}, bf16[4,2,64,1024]{3,2,1,0:T(8,128)(2,1)}, u32[]{:S(2)}) copy-start(bf16[4,2,64,1024]{3,2,1,0:T(8,128)(2,1)} %copy-done.4) | copy-start | bytes 3145732
  130.1 18.0 %copy-start.3 = (bf16[2,4,72,1024]{3,2,1,0:T(8,128)(2,1)S(1)}, bf16[2,4,72,1024]{3,2,1,0:T(8,128)(2,1)}, u32[]{:S(2)}) copy-start(bf16[2,4,72,1024]{3,2,1,0:T(8,128)(2,1)} %copy-done.2) | copy-start | bytes 3538948
  130.1 31.6 %collective-permute-start.25 = (bf16[4,2,64,1024]{3,2,1,0:T(8,128)(2,1)}, bf16[4,2,64,1024]{3,2,1,0:T(8,128)(2,1)}, u32[]{:S(2)}, u32[]{:S(2)}) collective-permute-start(bf16[4,2,64,1024]{3,2,1,0:T(8,128)(2,1)} %pad_maximum_fusion.2.refs_0_.refs_2_), channel_id=1, source_target_pairs={{0,1},{1,0},{2,3},{3,2},{4,5},{5,4},{6,7},{7,6},{8,9},{9,8},{10,11... | collective-permute-start | bytes 3145736 | tf_op jit(solution)/shard_map/ppermute | solution.py:47
  131.6 8.3 %copy-start.12 = (bf16[16,1,32,128]{3,2,1,0:T(8,128)(2,1)S(1)}, bf16[16,1,32,128]{3,2,1,0:T(8,128)(2,1)}, u32[]{:S(2)}) copy-start(bf16[16,1,32,128]{3,2,1,0:T(8,128)(2,1)} %copy-done.11) | copy-start | bytes 393220
  132.2 29.5 %collective-permute-start.24 = (bf16[2,128,1024]{2,1,0:T(8,128)(2,1)}, bf16[2,128,1024]{2,1,0:T(8,128)(2,1)}, u32[]{:S(2)}, u32[]{:S(2)}) collective-permute-start(bf16[2,128,1024]{2,1,0:T(8,128)(2,1)} %bitcast.183), channel_id=1, source_target_pairs={{0,2},{1,3},{2,4},{3,5},{4,6},{5,7},{6,0},{7,1},{8,10},{9,11},{10,... | collective-permute-start | bytes 1572872 | tf_op jit(solution)/shard_map/ppermute | solution.py:60
  134.8 26.8 %collective-permute-start.23 = (bf16[2,128,1024]{2,1,0:T(8,128)(2,1)}, bf16[2,128,1024]{2,1,0:T(8,128)(2,1)}, u32[]{:S(2)}, u32[]{:S(2)}) collective-permute-start(bf16[2,128,1024]{2,1,0:T(8,128)(2,1)} %bitcast.184), channel_id=1, source_target_pairs={{0,4},{1,5},{2,6},{3,7},{4,0},{5,1},{6,2},{7,3},{8,12},{9,13},{10,... | collective-permute-start | bytes 1572872 | tf_op jit(solution)/shard_map/ppermute | solution.py:60
  135.6 26.1 %collective-permute-start.22 = (bf16[2,128,1024]{2,1,0:T(8,128)(2,1)}, bf16[2,128,1024]{2,1,0:T(8,128)(2,1)}, u32[]{:S(2)}, u32[]{:S(2)}) collective-permute-start(bf16[2,128,1024]{2,1,0:T(8,128)(2,1)} %bitcast.185), channel_id=1, source_target_pairs={{0,6},{1,7},{2,0},{3,1},{4,2},{5,3},{6,4},{7,5},{8,14},{9,15},{10,... | collective-permute-start | bytes 1572872 | tf_op jit(solution)/shard_map/ppermute | solution.py:60
  140.2 21.5 %all-to-all-start.1 = ((f32[128,1,128]{2,1,0:T(1,128)}), f32[128,1,128]{2,1,0:T(1,128)S(1)}, u32[]{:S(2)}, u32[]{:S(2)}) async-start(f32[128,1,128]{2,1,0:T(1,128)} %broadcast_in_dim.152), calls=%async_computation.1 | async-start | bytes 131072 | tf_op jit(solution)/shard_map/all_to_all | solution.py:79
  148.1 15.8 %copy-start.26 = (pred[4,4]{1,0:T(4,128)(4,1)S(1)}, pred[4,4]{1,0:T(4,128)(4,1)}, u32[]{:S(2)}) copy-start(pred[4,4]{1,0:T(4,128)(4,1)} %iota_compare_fusion.6) | copy-start | bytes 52
  168.1 5.2 %copy-start.27 = (pred[64]{0:T(512)(128)(4,1)S(1)}, pred[64]{0:T(512)(128)(4,1)}, u32[]{:S(2)}) copy-start(pred[64]{0:T(512)(128)(4,1)} %get-tuple-element.144) | copy-start | bytes 196
  168.1 5.2 %copy-start.28 = (pred[64]{0:T(512)(128)(4,1)S(1)}, pred[64]{0:T(512)(128)(4,1)}, u32[]{:S(2)}) copy-start(pred[64]{0:T(512)(128)(4,1)} %get-tuple-element.143) | copy-start | bytes 196
  168.1 6.0 %copy-start.24 = (bf16[2,8,32,64]{3,2,1,0:T(8,128)(2,1)S(1)}, bf16[2,8,32,64]{3,2,1,0:T(8,128)(2,1)}, u32[]{:S(2)}) copy-start(bf16[2,8,32,64]{3,2,1,0:T(8,128)(2,1)} %fusion.34) | copy-start | bytes 196612
  168.1 7.0 %collective-permute-start.26 = (bf16[2,4,32,1024]{3,2,1,0:T(8,128)(2,1)}, bf16[2,4,32,1024]{3,2,1,0:T(8,128)(2,1)S(1)}, u32[]{:S(2)}, u32[]{:S(2)}) collective-permute-start(bf16[2,4,32,1024]{3,2,1,0:T(8,128)(2,1)} %get-tuple-element.98), channel_id=1, source_target_pairs={{0,8},{8,0},{16,24},{24,16},{32,40},{40,32},{48,56},{56,48},{64,72... | collective-permute-start | bytes 1572872 | tf_op jit(solution)/shard_map/ppermute | solution.py:39
  172.5 2.8 %collective-permute-start.27 = (bf16[2,4,32,1024]{3,2,1,0:T(8,128)(2,1)}, bf16[2,4,32,1024]{3,2,1,0:T(8,128)(2,1)}, u32[]{:S(2)}, u32[]{:S(2)}) collective-permute-start(bf16[2,4,32,1024]{3,2,1,0:T(8,128)(2,1)} %get-tuple-element.102), channel_id=1, source_target_pairs={{0,8},{8,0},{16,24},{24,16},{32,40},{40,32},{48,56},{56,48},{64,72... | collective-permute-start | bytes 1572872 | tf_op jit(solution)/shard_map/ppermute | solution.py:39
  176.6 13.4 %copy-start.25 = (s32[128,2]{0,1:T(2,128)S(1)}, s32[128,2]{0,1:T(2,128)}, u32[]{:S(2)}) copy-start(s32[128,2]{0,1:T(2,128)} %param.11) | copy-start | bytes 3076
  176.6 13.4 %copy-start.17 = (f32[128,64]{0,1:T(8,128)S(1)}, f32[128,64]{0,1:T(8,128)}, u32[]{:S(2)}) copy-start(f32[128,64]{0,1:T(8,128)} %param.10) | copy-start | bytes 98308
  177.7 25.7 %all-to-all-start.2 = ((bf16[8,2,32,1024]{3,2,1,0:T(8,128)(2,1)}), bf16[8,2,32,1024]{3,2,1,0:T(8,128)(2,1)S(1)}, u32[]{:S(2)}, u32[]{:S(2)}) async-start(bf16[8,2,32,1024]{3,2,1,0:T(8,128)(2,1)} %pad_maximum_fusion.3), calls=%async_computation.2 | async-start | bytes 2097152 | tf_op jit(solution)/shard_map/all_to_all | solution.py:51
  182.3 31.8 %collective-permute-start.28 = (f32[64,64]{1,0:T(8,128)S(1)}, f32[64,64]{1,0:T(8,128)S(1)}, u32[]{:S(2)}, u32[]{:S(2)}) collective-permute-start(f32[64,64]{1,0:T(8,128)S(1)} %convolution_add_fusion.1), channel_id=1, source_target_pairs={{0,0},{1,16},{2,32},{3,48},{4,64},{5,80},{6,96},{7,112},{8,1},{9,1... | collective-permute-start | bytes 49160 | tf_op jit(solution)/shard_map/ppermute | solution.py:457
  203.3 8.1 %copy-start.15 = (bf16[8192,64]{0,1:T(8,128)(2,1)S(1)}, bf16[8192,64]{0,1:T(8,128)(2,1)}, u32[]{:S(2)}) copy-start(bf16[8192,64]{0,1:T(8,128)(2,1)} %param.15) | copy-start | bytes 3145732
  204.5 11.3 %all-to-all-start.3 = ((bf16[8,8,1024]{2,1,0:T(8,128)(2,1)}), bf16[8,8,1024]{2,1,0:T(8,128)(2,1)S(1)}, u32[]{:S(2)}, u32[]{:S(2)}) async-start(bf16[8,8,1024]{2,1,0:T(8,128)(2,1)} %copy.158), calls=%async_computation.3 | async-start | bytes 262144 | tf_op jit(solution)/shard_map/all_to_all | solution.py:422
  (13 other events, 25.2 us)
